TPU v7x, 256 devices: a whole 4x4x8 slice. The times are simulated.
256 devices in a mesh: ctx: 64 (over z, y, core), head: 4 (over x).
Axes of the slice: x: 4, y: 4, z: 8, core: 2. Of those that a mesh axis runs over, the one named last changes fastest.
Arguments:
- query_rows: bfloat16 [8192, 4096], P('ctx', 'head'), may hold values from -300 to 300
- key_rows: bfloat16 [8192, 4096], P('ctx', 'head'), may hold values from -6 to 6
- value_rows: bfloat16 [8192, 4096], P('ctx', 'head'), may hold values from -6 to 6
- log_decay: float32 [32, 8192], P('head', 'ctx'), may hold values from -1 to 0, as said below
- step_size: float32 [32, 8192], P('head', 'ctx'), may hold values from 0.3 to 6.5
- band_mask: int32 [64, 5], P('ctx'), may hold values from 0 to 1, as said below
- cotangent: bfloat16 [8192, 4096], P('ctx', 'head'), may hold values from -6 to 6
Outputs:
- mixed_out: bfloat16 [8192, 4096], P('ctx', 'head')
- grad_queries: bfloat16 [8192, 4096], P('ctx', 'head')
- grad_keys: bfloat16 [8192, 4096], P('ctx', 'head')
- grad_values: bfloat16 [8192, 4096], P('ctx', 'head')
Inputs may be any that keep to these rules, and one draw needn't show every extreme that they name: `log_decay`: strictly negative. band_mask[b, j] = 1 lists the pair of query block b and key block b - j; column 0 is 1 in every row; a listed key block is never negative and is at least b - 4.
All inputs are finite; a program needn't handle non-finite values.
Results may differ from a plain program's by a relative error of at most 0.017.
Values may be sent and summed in bfloat16 or wider, within the bound.
A program may use at most 128 MiB of HBM per device.

v0:
```python
import jax
import jax.numpy as jnp
from jax import lax
from jax.sharding import PartitionSpec as P

HEAD_TOTAL = 32
HEAD_DIM = 128
BLK = 128
CYCLE = 4


def passed_along(block, axis, distance):
    devices = range(lax.axis_size(axis))
    route = [(i - distance, i) for i in devices if i - distance in devices]
    return lax.ppermute(block, axis, route)


def prefix_2(part, axis, combine, identity, reverse):
    count = lax.axis_size(axis)
    place = lax.axis_index(axis)
    ahead = count - 1 - place if reverse else place
    gathered = jax.tree.map(lambda a: lax.all_gather(a, axis), part)
    state = jax.tree.map(lambda a, e: jnp.zeros_like(a) + jnp.asarray(e, a.dtype), part, identity)

    def one(lap, state):
        source = count - 1 - lap if reverse else lap
        return combine(
            state, jax.tree.map(lambda a: lax.dynamic_index_in_dim(a, source, 0, False), gathered)
        )

    return lax.fori_loop(0, ahead, one, state)


def fetch_band(key_value, distance):
    return passed_along(key_value, "ctx", distance)


def return_grads(terms, distance):
    return passed_along(terms.astype(jnp.bfloat16), "ctx", -distance).astype(terms.dtype)


def chain_states(earlier, later):
    return (earlier[0] * later[0], later[0][:, None, None] * earlier[1] + later[1])


def body(query_rows, key_rows, value_rows, log_decay, step_size, band_mask, cotangent):
    highest = lax.Precision.HIGHEST
    tok_rows, feat_width = query_rows.shape
    head_count = log_decay.shape[0]
    head_width = feat_width // head_count
    blocks_dev = tok_rows // BLK
    score_scale = HEAD_DIM ** (-0.5)
    sources_count = CYCLE + 1

    def heads_first(rows):
        return rows.reshape(rows.shape[0], head_count, head_width).transpose(1, 0, 2)

    def tokens_first(headed):
        return headed.transpose(1, 0, 2).reshape(headed.shape[1], feat_width)

    key_value = jnp.stack([key_rows, value_rows])
    sources = [key_value]
    for distance in range(1, CYCLE + 1):
        sources.append(fetch_band(key_value, distance))
    band_rows = jnp.concatenate(sources, axis=1)
    query_blk = jnp.arange(blocks_dev)[:, None]
    key_cols = jnp.arange(sources_count * blocks_dev)[None, :]
    offset = key_cols // blocks_dev * blocks_dev + query_blk - key_cols % blocks_dev
    matches = offset[:, :, None] == jnp.arange(band_mask.shape[1])[None, None, :]
    listed = jnp.sum(jnp.where(matches, band_mask[:, None, :], 0), axis=-1) > 0
    token_mask = jnp.repeat(jnp.repeat(listed, BLK, axis=0), BLK, axis=1)
    query_h = heads_first(query_rows)
    key_h = heads_first(key_rows)
    value_h = heads_first(value_rows)
    cot_h = heads_first(cotangent)
    key_band = heads_first(band_rows[0])
    value_band = heads_first(band_rows[1])

    def per_head(operand):
        query_one, key_one, value_one, cot_one = operand
        scores = (
            jnp.einsum("td,ud->tu", query_one, key_one, preferred_element_type=jnp.float32)
            * score_scale
        )
        scores = jnp.where(token_mask, scores, -1e30)
        row_peak = jnp.max(scores, axis=-1, keepdims=True)
        exponent = jnp.exp(scores - row_peak)
        weights = exponent / jnp.sum(exponent, axis=-1, keepdims=True)
        weights_bf = weights.astype(jnp.bfloat16)
        attended = jnp.einsum(
            "tu,ud->td", weights_bf, value_one, preferred_element_type=jnp.float32
        )
        inner_prod = jnp.einsum("td,ud->tu", cot_one, value_one, preferred_element_type=jnp.float32)
        row_inner = jnp.sum(cot_one.astype(jnp.float32) * attended, axis=-1, keepdims=True)
        grad_scores = (score_scale * weights * (inner_prod - row_inner)).astype(jnp.bfloat16)
        grad_q = jnp.einsum("tu,ud->td", grad_scores, key_one, preferred_element_type=jnp.float32)
        grad_k = jnp.einsum("tu,td->ud", grad_scores, query_one, preferred_element_type=jnp.float32)
        grad_v = jnp.einsum("tu,td->ud", weights_bf, cot_one, preferred_element_type=jnp.float32)
        return (attended, grad_q, grad_k, grad_v)

    attended_h, att_dq, att_dk, att_dv = lax.map(per_head, (query_h, key_band, value_band, cot_h))
    band_terms = jnp.stack([tokens_first(att_dk), tokens_first(att_dv)])
    contrib = [
        band_terms[:, source * tok_rows : (source + 1) * tok_rows]
        for source in range(sources_count)
    ]
    returned = contrib[0]
    for distance in range(1, CYCLE + 1):
        returned = returned + return_grads(contrib[distance], distance)
    query_f = query_h.astype(jnp.float32)
    key_f = key_h.astype(jnp.float32)
    value_f = value_h.astype(jnp.float32)
    cot_f = cot_h.astype(jnp.float32)
    prefix = jnp.cumsum(log_decay, axis=1)
    last_sum = prefix[:, -1]
    fade_total = jnp.exp(last_sum)
    carry_weight = jnp.exp(last_sum[:, None] - prefix) * step_size
    local_state = jnp.einsum(
        "htn,htp->hnp", carry_weight[:, :, None] * key_f, value_f, precision=highest
    )
    identity = (jnp.ones_like(fade_total), jnp.zeros_like(local_state))
    entry_state = prefix_2((fade_total, local_state), "ctx", chain_states, identity, False)[1]
    token_position = jnp.arange(tok_rows)
    causal_mask = token_position[:, None] >= token_position[None, :]
    gap = jnp.where(causal_mask[None], prefix[:, :, None] - prefix[:, None, :], -jnp.inf)
    mixing = jnp.exp(gap) * step_size[:, None, :] * score_scale
    pair_prod = jnp.einsum("htn,hun->htu", query_h, key_h, preferred_element_type=jnp.float32)
    paired = mixing * pair_prod
    decay_now = jnp.exp(prefix)[:, :, None]
    ssd_out = jnp.einsum("htu,hup->htp", paired, value_f, precision=highest)
    ssd_out = ssd_out + score_scale * decay_now * jnp.einsum(
        "htn,hnp->htp", query_f, entry_state, precision=highest
    )
    channels = HEAD_TOTAL * HEAD_DIM
    squares = jnp.sum(ssd_out * ssd_out, axis=(0, 2))
    total_sq = lax.psum(squares, "head")
    root_mean = jnp.sqrt(total_sq / channels + 1e-05)[None, :, None]
    normed = ssd_out / root_mean
    cross_sum = lax.psum(jnp.sum(normed * cot_f, axis=(0, 2)), "head")
    d_ssd = (cot_f - normed * (cross_sum / channels)[None, :, None]) / root_mean
    own_back = score_scale * jnp.einsum(
        "htn,htp->hnp", decay_now * query_f, d_ssd, precision=highest
    )
    back_state = prefix_2((fade_total, own_back), "ctx", chain_states, identity, True)[1]
    inner_ssd = jnp.einsum("htp,hup->htu", d_ssd, value_f, precision=highest)
    weighted = mixing * inner_ssd
    ssd_dq = jnp.einsum("htu,hun->htn", weighted, key_f, precision=highest)
    ssd_dq = ssd_dq + score_scale * decay_now * jnp.einsum(
        "hnp,htp->htn", entry_state, d_ssd, precision=highest
    )
    ssd_dk = jnp.einsum("htu,htn->hun", weighted, query_f, precision=highest)
    ssd_dk = ssd_dk + carry_weight[:, :, None] * jnp.einsum(
        "hnp,hup->hun", back_state, value_f, precision=highest
    )
    ssd_dv = jnp.einsum("htu,htp->hup", paired, d_ssd, precision=highest)
    ssd_dv = ssd_dv + carry_weight[:, :, None] * jnp.einsum(
        "hnp,hun->hup", back_state, key_f, precision=highest
    )
    mixed_out = tokens_first(attended_h + normed).astype(jnp.bfloat16)
    grad_queries = tokens_first(att_dq + ssd_dq).astype(jnp.bfloat16)
    grad_keys = (returned[0] + tokens_first(ssd_dk)).astype(jnp.bfloat16)
    grad_values = (returned[1] + tokens_first(ssd_dv)).astype(jnp.bfloat16)
    return (mixed_out, grad_queries, grad_keys, grad_values)


def solution(mesh):
    return jax.shard_map(
        body,
        mesh=mesh,
        in_specs=(
            P("ctx", "head"),
            P("ctx", "head"),
            P("ctx", "head"),
            P("head", "ctx"),
            P("head", "ctx"),
            P("ctx", None),
            P("ctx", "head"),
        ),
        out_specs=(P("ctx", "head"), P("ctx", "head"), P("ctx", "head"), P("ctx", "head")),
        check_vma=False,
    )
```

profile of v0, /device:TPU:1, one launch (start us, length us, event | category | flops | bytes accessed | tf_op | source)
XLA Modules:
  0.0 589.0 jit_solution(1363545257655896976)
XLA Ops:
  9.2 2.7 fusion.57
  15.2 6.2 %collective-permute-start.2 = (bf16[2,128,1024]{1,2,0:T(8,128)(2,1)S(1)}, bf16[2,128,1024]{1,2,0:T(8,128)(2,1)S(1)}, u32[]{:S(2)}, u32[]{:S(2)}) collective-permute-start(bf16[2,128,1024]{1,2,0:T(8,128)(2,1)S(1)} %get-tuple-element.368), channel_id=1, source_target_pairs={{0,12},{4,16},{8,20},{12,24},{16,28},{20,32},{24,36},{28,40},{32,4... | collective-permute-start | bytes 1572872 | tf_op jit(solution)/shard_map/ppermute | solution.py:15
  21.4 3.1 collective-permute-start.1
  26.4 5.1 collective-permute-start.3
  34.7 156.2 %all-reduce = f32[512]{0:T(512)S(1)} all-reduce(f32[512]{0:T(512)S(1)} %dynamic-update-slice), channel_id=2, replica_groups=mesh['ctx'=64,'head'=4] {'ctx'}, use_global_device_ids=true, to_apply=%add | all-reduce | flops 512 | bytes 4096
  198.8 3.1 fusion.79
  201.8 46.7 %while.45 = (s32[]{:T(128)}, f32[8,128,128]{1,2,0:T(8,128)S(1)}, f32[8,128,128]{1,2,0:T(8,128)}, f32[8,640,128]{2,1,0:T(8,128)}, f32[8,640,128]{2,1,0:T(8,128)},...) while((s32[]{:T(128)}, f32[8,128,128]{1,2,0:T(8,128)S(1)}, ...), condition=%wide.region_5.6_spmd.clone, body=%wide.region_1.5_spmd.clone.sunk | while | flops 127270528 | bytes 3879545 | solution.py:101
  250.5 8.5 %psum.14 = f32[128]{0:T(128)S(1)} all-reduce(f32[128]{0:T(128)S(1)} %get-tuple-element.373), channel_id=1, replica_groups=mesh['ctx'=64,'head'=4] {'head'}, use_global_device_ids=true, to_apply=%region_10.11 | all-reduce | flops 128 | bytes 1024 | tf_op jit(solution)/shard_map/psum | solution.py:136
  259.8 6.2 %psum.15 = f32[128]{0:T(128)S(1)} all-reduce(f32[128]{0:T(128)S(1)} %get-tuple-element.366), channel_id=1, replica_groups=mesh['ctx'=64,'head'=4] {'head'}, use_global_device_ids=true, to_apply=%region_12.13 | all-reduce | flops 128 | bytes 1024 | tf_op jit(solution)/shard_map/psum | solution.py:139
  266.1 3.2 convolution_multiply_fusion.1
  269.3 3.1 copy.113
  272.3 2.6 stack_reshape.7
  274.9 4.8 copy.112
  279.7 3.8 stack_reshape.6
  283.5 2.0 constant_dynamic-update-slice_fusion.6
  286.1 2.0 copy-done
  289.3 4.9 collective-permute-start.4
  298.9 2.4 collective-permute-done.4
  301.3 10.3 %collective-permute-done.7 = bf16[2,128,1024]{2,1,0:T(8,128)(2,1)} collective-permute-done((bf16[2,128,1024]{2,1,0:T(8,128)(2,1)}, bf16[2,128,1024]{2,1,0:T(8,128)(2,1)}, u32[]{:S(2)}, u32[]{:S(2)}) %collective-permute-start.7) | collective-permute-done | bytes 524320 | tf_op jit(solution)/shard_map/ppermute | solution.py:15
  311.6 5.5 collective-permute-done.6
  317.1 16.9 %collective-permute-done.5 = bf16[2,128,1024]{2,1,0:T(8,128)(2,1)} collective-permute-done((bf16[2,128,1024]{2,1,0:T(8,128)(2,1)S(1)}, bf16[2,128,1024]{2,1,0:T(8,128)(2,1)}, u32[]{:S(2)}, u32[]{:S(2)}) %collective-permute-start.5) | collective-permute-done | bytes 524320 | tf_op jit(solution)/shard_map/ppermute | solution.py:15
  334.0 2.2 fusion.48
  342.7 159.3 %all-gather.8.cloned.1.call-done = f32[512,128,128]{2,1,0:T(8,128)} async-done(((f32[8,128,128]{2,1,0:T(8,128)}), f32[512,128,128]{2,1,0:T(8,128)}) %all-gather.8.cloned.1.call-update) | async-done | bytes 33554448 | tf_op jit(solution)/shard_map/all_gather | solution.py:22
  502.0 76.4 %while.44 = (s32[]{:T(128)}, f32[8,128,128]{2,1,0:T(8,128)S(1)}, s32[]{:T(128)}, f32[64,8]{1,0:T(8,128)S(1)}, f32[64,8,128,128]{3,2,1,0:T(8,128)}, /*index=5*/s32[]{:T(128)}, s32[]{:T(128)}, s32[]{:T(128)}, s32[]{:T(128)}) while((s32[]{:T(128)}, f32[8,128,128]{2,1,0:T(8,128)S(1)}, s32[]{:T(128)}, f32[64,8]{1,0:T(8,128)S(1)}, ...), condition=%wide.region_14.15_spmd, body=%wide.region_13.14_spmd.sunk | while | flops 262150 | bytes 1573115 | solution.py:31
  (298 shorter events, 159.1 us)
Async XLA Ops:
  7.2 24.6 %copy-start.1 = (bf16[128,1024]{1,0:T(8,128)(2,1)S(1)}, bf16[128,1024]{1,0:T(8,128)(2,1)}, u32[]{:S(2)}) copy-start(bf16[128,1024]{1,0:T(8,128)(2,1)} %param.15) | copy-start | bytes 786436
  7.2 24.4 %copy-start.18 = (bf16[128,1024]{1,0:T(8,128)(2,1)S(1)}, bf16[128,1024]{1,0:T(8,128)(2,1)}, u32[]{:S(2)}) copy-start(bf16[128,1024]{1,0:T(8,128)(2,1)} %param.13) | copy-start | bytes 786436
  7.2 241.4 %all-gather.6.cloned.1.call-start = ((), (), s32[]{:S(2)}) async-start(), calls=%async_computation | async-start | bytes 34078720 | tf_op jit(solution)/shard_map/all_gather | solution.py:22
  9.2 22.6 %copy-start.3 = (bf16[128,1024]{1,0:T(8,128)(2,1)S(1)}, bf16[128,1024]{1,0:T(8,128)(2,1)}, u32[]{:S(2)}) copy-start(bf16[128,1024]{1,0:T(8,128)(2,1)} %param.14) | copy-start | bytes 786436
  9.2 22.6 %copy-start.19 = (f32[8,128]{1,0:T(8,128)S(1)}, f32[8,128]{1,0:T(8,128)}, u32[]{:S(2)}) copy-start(f32[8,128]{1,0:T(8,128)} %param.17) | copy-start | bytes 12292
  11.9 490.1 %all-gather.8.cloned.1.call-start = ((), (), s32[]{:S(2)}) async-start(), calls=%async_computation.1 | async-start | bytes 34078720 | tf_op jit(solution)/shard_map/all_gather | solution.py:22
  14.2 18.7 %copy-start.21 = (s32[1,5]{1,0:T(1,128)S(1)}, s32[1,5]{1,0:T(1,128)}, u32[]{:S(2)}) copy-start(s32[1,5]{1,0:T(1,128)} %param.18) | copy-start | bytes 64
  14.2 18.9 %copy-start.22 = (u32[256]{0:T(256)S(1)}, u32[256]{0:T(256)}, u32[]{:S(2)}) copy-start(u32[256]{0:T(256)} %constant.128) | copy-start | bytes 3076
  15.2 180.7 %collective-permute-start.2 = (bf16[2,128,1024]{1,2,0:T(8,128)(2,1)S(1)}, bf16[2,128,1024]{1,2,0:T(8,128)(2,1)S(1)}, u32[]{:S(2)}, u32[]{:S(2)}) collective-permute-start(bf16[2,128,1024]{1,2,0:T(8,128)(2,1)S(1)} %get-tuple-element.368), channel_id=1, source_target_pairs={{0,12},{4,16},{8,20},{12,24},{16,28},{20,32},{24,36},{28,40},{32,4... | collective-permute-start | bytes 1572872 | tf_op jit(solution)/shard_map/ppermute | solution.py:15
  21.4 172.6 %collective-permute-start.1 = (bf16[2,128,1024]{1,2,0:T(8,128)(2,1)S(1)}, bf16[2,128,1024]{1,2,0:T(8,128)(2,1)}, u32[]{:S(2)}, u32[]{:S(2)}) collective-permute-start(bf16[2,128,1024]{1,2,0:T(8,128)(2,1)S(1)} %get-tuple-element.368), channel_id=1, source_target_pairs={{0,8},{4,12},{8,16},{12,20},{16,24},{20,28},{24,32},{28,36},{32,40... | collective-permute-start | bytes 1572872 | tf_op jit(solution)/shard_map/ppermute | solution.py:15
  24.5 167.6 %collective-permute-start = (bf16[2,128,1024]{1,2,0:T(8,128)(2,1)S(1)}, bf16[2,128,1024]{1,2,0:T(8,128)(2,1)}, u32[]{:S(2)}, u32[]{:S(2)}) collective-permute-start(bf16[2,128,1024]{1,2,0:T(8,128)(2,1)S(1)} %get-tuple-element.368), channel_id=1, source_target_pairs={{0,4},{4,8},{8,12},{12,16},{16,20},{20,24},{24,28},{28,32},{32,36}... | collective-permute-start | bytes 1572872 | tf_op jit(solution)/shard_map/ppermute | solution.py:15
  26.4 170.4 %collective-permute-start.3 = (bf16[2,128,1024]{1,2,0:T(8,128)(2,1)S(1)}, bf16[2,128,1024]{1,2,0:T(8,128)(2,1)}, u32[]{:S(2)}, u32[]{:S(2)}) collective-permute-start(bf16[2,128,1024]{1,2,0:T(8,128)(2,1)S(1)} %get-tuple-element.368), channel_id=1, source_target_pairs={{0,16},{4,20},{8,24},{12,28},{16,32},{20,36},{24,40},{28,44},{32,4... | collective-permute-start | bytes 1572872 | tf_op jit(solution)/shard_map/ppermute | solution.py:15
  32.2 164.6 %copy-start.14 = (f32[8,128,128]{2,1,0:T(8,128)}, f32[8,128,128]{2,1,0:T(8,128)S(1)}, u32[]{:S(2)}) copy-start(f32[8,128,128]{2,1,0:T(8,128)S(1)} %convolution_multiply_fusion.3) | copy-start | bytes 1572868
  248.6 10.4 %copy-start.9 = (bf16[8,128,128]{1,2,0:T(8,128)(2,1)}, bf16[8,128,128]{1,2,0:T(8,128)(2,1)S(1)}, u32[]{:S(2)}) copy-start(bf16[8,128,128]{1,2,0:T(8,128)(2,1)S(1)} %get-tuple-element.597) | copy-start | bytes 786436
  259.8 9.4 %copy-start.5 = (f32[8,640,128]{2,1,0:T(8,128)S(1)}, f32[8,640,128]{2,1,0:T(8,128)}, u32[]{:S(2)}) copy-start(f32[8,640,128]{2,1,0:T(8,128)} %get-tuple-element.191) | copy-start | bytes 7864324
  288.1 10.1 %copy-start.4 = (bf16[128,1024]{1,0:T(8,128)(2,1)S(1)}, bf16[128,1024]{1,0:T(8,128)(2,1)}, u32[]{:S(2)}) copy-start(bf16[128,1024]{1,0:T(8,128)(2,1)} %param.14) | copy-start | bytes 786436
  289.3 46.9 %copy-start.13 = (bf16[8,128,128]{1,2,0:T(8,128)(2,1)S(1)}, bf16[8,128,128]{1,2,0:T(8,128)(2,1)}, u32[]{:S(2)}) copy-start(bf16[8,128,128]{1,2,0:T(8,128)(2,1)} %get-tuple-element.367) | copy-start | bytes 786436
  289.3 12.0 %collective-permute-start.4 = (bf16[2,128,1024]{2,1,0:T(8,128)(2,1)}, bf16[2,128,1024]{2,1,0:T(8,128)(2,1)S(1)}, u32[]{:S(2)}, u32[]{:S(2)}) collective-permute-start(bf16[2,128,1024]{2,1,0:T(8,128)(2,1)} %get-tuple-element.358), channel_id=1, source_target_pairs={{4,0},{8,4},{12,8},{16,12},{20,16},{24,20},{28,24},{32,28},{36,32}... | collective-permute-start | bytes 1572872 | tf_op jit(solution)/shard_map/ppermute | solution.py:15
  294.2 17.4 %collective-permute-start.7 = (bf16[2,128,1024]{2,1,0:T(8,128)(2,1)}, bf16[2,128,1024]{2,1,0:T(8,128)(2,1)}, u32[]{:S(2)}, u32[]{:S(2)}) collective-permute-start(bf16[2,128,1024]{2,1,0:T(8,128)(2,1)} %get-tuple-element.359), channel_id=1, source_target_pairs={{16,0},{20,4},{24,8},{28,12},{32,16},{36,20},{40,24},{44,28},{48,3... | collective-permute-start | bytes 1572872 | tf_op jit(solution)/shard_map/ppermute | solution.py:15
  295.5 21.5 %collective-permute-start.6 = (bf16[2,128,1024]{2,1,0:T(8,128)(2,1)}, bf16[2,128,1024]{2,1,0:T(8,128)(2,1)}, u32[]{:S(2)}, u32[]{:S(2)}) collective-permute-start(bf16[2,128,1024]{2,1,0:T(8,128)(2,1)} %get-tuple-element.360), channel_id=1, source_target_pairs={{12,0},{16,4},{20,8},{24,12},{28,16},{32,20},{36,24},{40,28},{44,3... | collective-permute-start | bytes 1572872 | tf_op jit(solution)/shard_map/ppermute | solution.py:15
  296.8 37.1 %collective-permute-start.5 = (bf16[2,128,1024]{2,1,0:T(8,128)(2,1)S(1)}, bf16[2,128,1024]{2,1,0:T(8,128)(2,1)}, u32[]{:S(2)}, u32[]{:S(2)}) collective-permute-start(bf16[2,128,1024]{2,1,0:T(8,128)(2,1)S(1)} %get-tuple-element.361), channel_id=1, source_target_pairs={{8,0},{12,4},{16,8},{20,12},{24,16},{28,20},{32,24},{36,28},{40,32... | collective-permute-start | bytes 1572872 | tf_op jit(solution)/shard_map/ppermute | solution.py:15
  298.1 38.9 %copy-start.2 = (bf16[128,1024]{1,0:T(8,128)(2,1)S(1)}, bf16[128,1024]{1,0:T(8,128)(2,1)}, u32[]{:S(2)}) copy-start(bf16[128,1024]{1,0:T(8,128)(2,1)} %param.15) | copy-start | bytes 786436
  298.1 38.9 %copy-start.7 = (f32[8,128,128]{1,2,0:T(8,128)S(1)}, f32[8,128,128]{1,2,0:T(8,128)}, u32[]{:S(2)}) copy-start(f32[8,128,128]{1,2,0:T(8,128)} %copy-done.6) | copy-start | bytes 1572868
  301.3 15.7 %copy-start.17 = (bf16[2,128,1024]{2,1,0:T(8,128)(2,1)}, bf16[2,128,1024]{2,1,0:T(8,128)(2,1)S(1)}, u32[]{:S(2)}) copy-start(bf16[2,128,1024]{2,1,0:T(8,128)(2,1)S(1)} %collective-permute-done.4) | copy-start | bytes 1572868
  (9 other events, 25.7 us)
Sparse Core Ops, SparseCore 0:
  12.0 174.5 all-gather.5
  269.4 232.5 all-gather.7
where the time goes:
time: 593 us; the launch traced here: 589 us
  waiting for transfers between devices  194 us (33%)
  blocking collectives  171 us (29%)
  other arithmetic  84.4 us (14%)
  matrix products  58.2 us (10%)
  local copies, waits for them, and re-layouts  38.6 us (7%)
  starting transfers between devices  25.2 us (4%)
  between operations  15.2 us (3%)
    all_gather x2, waiting for transfers between devices, prefix_2(): gathered = jax.tree.map(lambda a: lax.all_gather(a, axis), part)  159 us
    unnamed x1, blocking collectives  156 us
    add x63, other arithmetic, chain_states(): later[0][:, None, None] * earlier[1] + later[1]  75.1 us
    ppermute x8, waiting for transfers between devices, passed_along(): return lax.ppermute(block, axis, route)  35.1 us
    ppermute x8, starting transfers between devices, passed_along(): return lax.ppermute(block, axis, route)  25.1 us
    unnamed x61, local copies, waits for them, and re-layouts  16.6 us
  transfers between devices with their start and end apart: 10, of which 5 were waited for; matrix products, arithmetic and copies ran while one was open for 15% of the time, Pallas kernels for 0%

commit v1 on v0

v1 whole, which is shorter than its diff:
```python
import functools

import jax
import jax.numpy as jnp
from jax import lax
from jax.experimental import pallas as pl
from jax.experimental.pallas import tpu as pltpu
from jax.sharding import PartitionSpec as P

MESH = pl.DeviceIdType.MESH
HIGHEST = lax.Precision.HIGHEST
F32 = jnp.float32
BF16 = jnp.bfloat16
D = 128
HH = 4
HW = HH * D
T2 = 256
W3 = 768
CHANNELS = 4096
SCALE = D ** (-0.5)
BIG = 1e30


def nn(a, b):
    return lax.dot_general(a, b, (((1,), (0,)), ((), ())), preferred_element_type=F32)


def nt(a, b):
    return lax.dot_general(a, b, (((1,), (1,)), ((), ())), preferred_element_type=F32)


def tn(a, b):
    return lax.dot_general(a, b, (((0,), (0,)), ((), ())), preferred_element_type=F32)


def kernel(
    nc, nx,
    q_ref, k_ref, v_ref, g_ref, ld_ref, st_ref, bm_ref,
    om_ref, oq_ref, ok_ref, ov_ref,
    kb, vb, qb, gb, ldb, stb, mk, f_out, f_in, l_out, l_in, e_out, e_in,
    o_in, o_out, b_out, b_in, xs, stat, rows, cols, bias, big,
    mix, mixt, pairt, ssd, dss, att, dq, dk, dv, outs,
    ssem, rsem, lsem,
):
    me = lax.axis_index("ctx")
    x = lax.axis_index("head")
    c = me // 2
    j = me % 2
    part = 512 // nc

    def dev(chip, core, xx):
        return (lax.rem(chip, nc) * 2 + core, xx)

    def order(n):
        half = (n + 1) // 2
        return nc // 2 + jnp.where(n % 2 == 0, half, -half)

    barrier = pltpu.get_barrier_semaphore()

    def greet(n, carry):
        pl.semaphore_signal(barrier, 1, device_id=dev(c + order(n), j, x), device_id_type=MESH)
        return carry

    lax.fori_loop(0, nc - 1, greet, 0)
    greeted = nc - 1
    for other in (dev(c + 1, 1 - j, x), dev(c + nc - 1, 1 - j, x), dev(c, 1 - j, x)):
        pl.semaphore_signal(barrier, 1, device_id=other, device_id_type=MESH)
        greeted += 1
    for step in range(1, nx):
        for core in range(2):
            pl.semaphore_signal(
                barrier, 1, device_id=dev(c, core, lax.rem(x + step, nx)), device_id_type=MESH
            )
            greeted += 1

    sends = []
    count = {"s": 0, "r": 0}

    def slots(kind, n):
        at = count[kind]
        count[kind] += n
        return at

    def remote(src, dst, recv, target):
        copy = pltpu.make_async_remote_copy(
            src_ref=src, dst_ref=dst, send_sem=ssem.at[slots("s", 1)], recv_sem=rsem.at[recv],
            device_id=target, device_id_type=MESH,
        )
        sends.append((copy, src))
        copy.start()

    def arrived(ref, recv):
        pltpu.make_async_copy(ref, ref, rsem.at[recv]).wait()

    mine = pl.ds(pl.multiple_of(j * HW, HW), HW)
    other_half = pl.ds(pl.multiple_of((1 - j) * HW, HW), HW)
    local = []
    for n, (src, dst, slot) in enumerate(
        ((k_ref, kb, 2), (v_ref, vb, 2), (q_ref, qb, 0), (g_ref, gb, 0))
    ):
        copy = pltpu.make_async_copy(src.at[:, mine], dst.at[slot, j], lsem.at[n])
        copy.start()
        local.append(copy)
    ldb[j] = ld_ref[...]
    stb[j] = st_ref[...]
    listed = bm_ref[...].astype(F32)
    mk[j] = jnp.concatenate(
        [jnp.broadcast_to(listed[:, n : n + 1], (1, D)) for n in range(5)]
        + [jnp.zeros((3, D), F32)],
        axis=0,
    )

    pl.semaphore_wait(barrier, greeted)

    mate = dev(c, 1 - j, x)
    small = slots("r", 3)
    remote(ldb.at[j], ldb.at[j], small, mate)
    remote(stb.at[j], stb.at[j], small + 1, mate)
    remote(mk.at[j], mk.at[j], small + 2, mate)
    swap = slots("r", 4)
    for n, (src, dst, slot) in enumerate(
        ((k_ref, kb, 2), (v_ref, vb, 2), (q_ref, qb, 0), (g_ref, gb, 0))
    ):
        remote(src.at[:, other_half], dst.at[slot, j], swap + n, mate)
    first = slots("r", 8)
    for n, (src, dst, step) in enumerate(
        ((k_ref, kb, 1), (q_ref, qb, nc - 1), (v_ref, vb, 1), (g_ref, gb, nc - 1))
    ):
        for core in range(2):
            remote(
                src.at[:, pl.ds(core * HW, HW)], dst.at[1, j], first + 2 * n + j,
                dev(c + step, core, x),
            )

    for n, ref in enumerate((ldb, stb, mk)):
        arrived(ref.at[1 - j], small + n)
    low = j == 0
    pair = []
    for ref in (ldb, stb):
        wide = jnp.concatenate([ref[0], ref[1]], axis=1)
        pair.append(jnp.where(low, wide[0:HH], wide[HH : 2 * HH]))
    decay, step_row = pair
    at_row = lax.broadcasted_iota(jnp.int32, (T2, T2), 0)
    at_col = lax.broadcasted_iota(jnp.int32, (T2, T2), 1)
    upper = (at_row <= at_col).astype(F32)
    prefix = lax.dot_general(
        jnp.concatenate([decay, decay], axis=0), upper, (((1,), (0,)), ((), ())),
        precision=HIGHEST, preferred_element_type=F32,
    )[0:HH]
    last = prefix[:, T2 - 1 : T2]
    carry_row = jnp.exp(last - prefix) * step_row
    packed = jnp.concatenate([prefix, step_row, carry_row, jnp.exp(prefix)], axis=0)
    rows[...] = packed
    cols[...] = jnp.transpose(packed)
    last_wide = jnp.broadcast_to(last, (HH, D))
    fade_tile = jnp.concatenate([last_wide, last_wide], axis=0)
    f_out[...] = fade_tile
    f_in[pl.ds(c, 1)] = fade_tile[None]

    a2a = []

    def exchange(src_of, dst_of):
        s_at, r_at = slots("s", 1), slots("r", 1)

        def one(n, carry):
            chip = lax.rem(c + order(n), nc)
            pltpu.make_async_remote_copy(
                src_ref=src_of(chip), dst_ref=dst_of(c), send_sem=ssem.at[s_at],
                recv_sem=rsem.at[r_at], device_id=(chip * 2 + j, x), device_id_type=MESH,
            ).start()
            return carry

        lax.fori_loop(0, nc - 1, one, 0)
        return s_at, r_at

    def own(chip):
        return pl.ds(pl.multiple_of(chip * part, part), part)

    f_sem = exchange(lambda chip: f_out, lambda sender: f_in.at[sender])

    for n in range(4):
        local[n].wait()
    arrived(kb.at[2, 1 - j], swap)
    arrived(vb.at[2, 1 - j], swap + 1)

    def head(ref, slot, h):
        return ref[slot, :, :, h * D : (h + 1) * D].reshape(T2, D)

    def band(ref, h):
        return ref[:, :, :, h * D : (h + 1) * D].reshape(W3, D)

    for h in range(HH):
        weighted = (cols[:, 8 + h : 9 + h] * head(kb, 2, h).astype(F32)).astype(BF16)
        l_out[h * D : (h + 1) * D, :] = tn(weighted, head(vb, 2, h)).astype(BF16)
    l_in[pl.ds(c, 1)] = l_out[own(c), :][None]
    l_sem = exchange(lambda chip: l_out.at[own(chip)], lambda sender: l_in.at[sender])

    blank = jnp.full((1, D), BIG, F32)
    for core in range(2):
        line = []
        for dist in (2, 1, 0):
            for core_k in range(2):
                off = 2 * dist + core - core_k
                line.append((1.0 - mk[core, off : off + 1, :]) * BIG if 0 <= off < 5 else blank)
        bias[core : core + 1, :] = jnp.concatenate(line, axis=1) * -1.0

    arrived(qb.at[0, 1 - j], swap + 2)
    arrived(gb.at[0, 1 - j], swap + 3)
    for h in range(HH):
        q, k, v = head(qb, 0, h), head(kb, 2, h), head(vb, 2, h)
        p_row, p_col = rows[h : h + 1, :], cols[:, h : h + 1]
        m = jnp.exp(jnp.where(at_row >= at_col, p_col - p_row, -BIG)) * (
            rows[4 + h : 5 + h, :] * SCALE
        )
        mix[h] = m
        ssd[h] = nn((m * nt(q, k)).astype(BF16), v)
        mt = jnp.exp(jnp.where(at_row <= at_col, p_row - p_col, -BIG)) * (
            cols[:, 4 + h : 5 + h] * SCALE
        )
        mixt[h] = mt
        pairt[h] = (mt * nt(k, q)).astype(BF16)

    second = slots("r", 8)
    for n, (buf, step) in enumerate(((kb, 1), (qb, nc - 1), (vb, 1), (gb, nc - 1))):
        far = 0 if step == 1 else 2
        for core in range(2):
            arrived(buf.at[1, core], first + 2 * n + core)
            remote(buf.at[1, core], buf.at[far, core], second + 2 * n + core, dev(c + step, j, x))

    def total(ref):
        return ref.at[pl.ds(0, nc - 1)]

    head_of = c * part // D
    arrived(total(f_in), f_sem[1])
    arrived(total(l_in), l_sem[1])

    def scan(src, dst, reverse):
        def one(n, run):
            chip = nc - 1 - n if reverse else n
            dst[pl.ds(chip, 1)] = run.astype(BF16)[None]
            fade = jnp.exp(f_in[pl.ds(chip, 1), pl.ds(head_of, 1), :][0])
            return fade * run + src[pl.ds(chip, 1)][0].astype(F32)

        lax.fori_loop(0, nc, one, jnp.zeros((part, D), F32), unroll=True)

    scan(l_in, e_out, False)
    e_sem = exchange(lambda chip: e_out.at[chip], lambda sender: e_in.at[own(sender)])
    e_in[own(c), :] = e_out[pl.ds(c, 1)][0]

    rest = e_in.at[pl.ds(0, 512 - part)]
    arrived(rest, e_sem[1])
    squares = jnp.zeros((T2, D), F32)
    inner = jnp.zeros((T2, D), F32)
    for h in range(HH):
        state = e_in[h * D : (h + 1) * D, :]
        y = ssd[h] + (SCALE * cols[:, 12 + h : 13 + h]) * nn(head(qb, 0, h), state)
        ssd[h] = y
        squares = squares + y * y
        inner = inner + y * head(gb, 0, h).astype(F32)
    ones = jnp.ones((8, D), F32)

    def across(a):
        return lax.dot_general(
            ones, a, (((1,), (1,)), ((), ())), precision=HIGHEST, preferred_element_type=F32
        )

    sums = jnp.concatenate([across(squares)[0:4], across(inner)[0:4]], axis=0)
    here = x * 2 + j
    xs[pl.ds(here, 1)] = sums[None]
    x_s, x_r = slots("s", 1), slots("r", 1)
    for step in range(nx):
        for core in range(2):
            if step == 0 and core == 0:
                continue
            pltpu.make_async_remote_copy(
                src_ref=xs.at[here], dst_ref=xs.at[here], send_sem=ssem.at[x_s],
                recv_sem=rsem.at[x_r],
                device_id=dev(c, (j + core) % 2, lax.rem(x + step, nx)), device_id_type=MESH,
            ).start()

    columns = []

    def query_side(h):
        q, g = head(qb, 0, h), head(gb, 0, h)
        k, v = band(kb, h), band(vb, h)
        s = nt(q, k) * SCALE
        s = (s.reshape(2, D, W3) + bias[0:2, :][:, None, :]).reshape(T2, W3)
        peak = jnp.max(s, axis=-1, keepdims=True)
        e = jnp.exp(s - peak)
        inv = 1.0 / jnp.sum(e, axis=-1, keepdims=True)
        w = e * inv
        a = nn(w.astype(BF16), v)
        att[h] = a
        row_inner = jnp.sum(g.astype(F32) * a, axis=-1, keepdims=True)
        gs = (SCALE * w * (nt(g, v) - row_inner)).astype(BF16)
        dq[h] = nn(gs, k)
        columns.append((peak, inv, row_inner))

    for core in range(2):
        arrived(kb.at[0, core], second + core)
        arrived(vb.at[0, core], second + 4 + core)
    query_side(0)
    query_side(1)

    arrived(xs.at[pl.ds(0, 2 * nx - 1)], x_r)
    both = xs[0]
    for n in range(1, 2 * nx):
        both = both + xs[n]
    inv_root = 1.0 / jnp.sqrt(both[0:4] / CHANNELS + 1e-05)
    cross = both[4:8] * inv_root / CHANNELS
    turned = jnp.transpose(jnp.concatenate([inv_root, inv_root * inv_root * cross], axis=0))
    root_col, slope_col = turned[:, 0:1], turned[:, 4:5]
    for h in range(HH):
        g = head(gb, 0, h).astype(F32)
        y = ssd[h]
        d = (g * root_col - y * slope_col).astype(BF16)
        dss[h] = d
        faded = (cols[:, 12 + h : 13 + h] * head(qb, 0, h).astype(F32)).astype(BF16)
        o_out[h * D : (h + 1) * D, :] = (SCALE * tn(faded, d)).astype(BF16)
        ssd[h] = y * root_col
    o_in[pl.ds(c, 1)] = o_out[own(c), :][None]
    o_sem = exchange(lambda chip: o_out.at[own(chip)], lambda sender: o_in.at[sender])

    query_side(2)
    query_side(3)

    lane = lax.broadcasted_iota(jnp.int32, (T2, D), 1)
    grid = jnp.zeros((T2, D), F32)
    for kind in range(3):
        for h in range(HH):
            grid = jnp.where(lane == kind * HH + h, columns[h][kind], grid)
    stat[0, 0:16, :] = jnp.transpose(grid)[0:16]
    stat[0, 16:24, :] = jnp.concatenate([mk[0], mk[1]], axis=1)
    stat_r = slots("r", 2)
    for dist in (1, 2):
        remote(stat.at[0], stat.at[dist], stat_r + dist - 1, dev(c + nc - dist, j, x))

    out_sends = []
    out_local = []
    out_r = slots("r", 4)

    def emit(n, ref):
        copy = pltpu.make_async_copy(outs.at[n, j], ref.at[:, mine], lsem.at[4 + n])
        copy.start()
        out_local.append(copy)
        far = pltpu.make_async_remote_copy(
            src_ref=outs.at[n, 1 - j], dst_ref=ref.at[:, mine], send_sem=ssem.at[slots("s", 1)],
            recv_sem=rsem.at[out_r + n], device_id=mate, device_id_type=MESH,
        )
        far.start()
        out_sends.append(far)

    def put(n, h, value):
        outs[n, :, :, h * D : (h + 1) * D] = value.astype(BF16).reshape(2, D, D)

    for h in range(HH):
        q, k, v, d = head(qb, 0, h), head(kb, 2, h), head(vb, 2, h), dss[h]
        state = e_in[h * D : (h + 1) * D, :]
        put(0, h, att[h] + ssd[h])
        grad = nn((mix[h] * nt(d, v)).astype(BF16), k)
        grad = grad + (SCALE * cols[:, 12 + h : 13 + h]) * nt(d, state)
        put(1, h, dq[h] + grad)
        dk[h] = nn((mixt[h] * nt(v, d)).astype(BF16), q)
        dv[h] = nn(pairt[h], d)
    emit(0, om_ref)
    emit(1, oq_ref)

    arrived(total(o_in), o_sem[1])
    scan(o_in, b_out, True)
    b_sem = exchange(lambda chip: b_out.at[chip], lambda sender: b_in.at[own(sender)])
    b_in[own(c), :] = b_out[pl.ds(c, 1)][0]

    for dist in (1, 2):
        arrived(stat.at[dist], stat_r + dist - 1)
    for core in range(2):
        arrived(qb.at[2, core], second + 2 + core)
        arrived(gb.at[2, core], second + 6 + core)
    for core_k in range(2):
        line = []
        for dist in range(3):
            here_ok = c + dist < nc
            for core in range(2):
                off = 2 * dist + core - core_k
                if 0 <= off < 5:
                    listed = stat[dist, 16 + off : 17 + off, core * D : (core + 1) * D]
                    line.append(jnp.where(here_ok, (1.0 - listed) * BIG, BIG))
                else:
                    line.append(blank)
        big[core_k : core_k + 1, :] = jnp.concatenate(line, axis=1)
    for h in range(HH):
        q, g = band(qb, h), band(gb, h)
        k, v = head(kb, 2, h), head(vb, 2, h)
        peak, inv, row_inner = [
            jnp.concatenate([stat[n, kind * HH + h : kind * HH + h + 1, :] for n in range(3)], axis=1)
            for kind in range(3)
        ]
        shift = peak + big[0:2, :]
        s = nt(k, q) * SCALE
        w = jnp.exp((s.reshape(2, D, W3) - shift[:, None, :]).reshape(T2, W3)) * inv
        dv[h] = dv[h] + nn(w.astype(BF16), g)
        gs = (SCALE * w * (nt(v, g) - row_inner)).astype(BF16)
        dk[h] = dk[h] + nn(gs, q)

    arrived(b_in.at[pl.ds(0, 512 - part)], b_sem[1])
    for h in range(HH):
        state = b_in[h * D : (h + 1) * D, :]
        weight = cols[:, 8 + h : 9 + h]
        put(2, h, dk[h] + weight * nt(head(vb, 2, h), state))
        put(3, h, dv[h] + weight * nn(head(kb, 2, h), state))
    emit(2, ok_ref)
    emit(3, ov_ref)

    for copy, _ in sends:
        copy.wait_send()
    pltpu.make_async_copy(total(f_in), total(f_in), ssem.at[f_sem[0]]).wait()
    for ref, sem in ((l_in, l_sem), (e_out, e_sem), (o_in, o_sem), (b_out, b_sem)):
        pltpu.make_async_copy(total(ref), total(ref), ssem.at[sem[0]]).wait()
    rest_x = xs.at[pl.ds(0, 2 * nx - 1)]
    pltpu.make_async_copy(rest_x, rest_x, ssem.at[x_s]).wait()
    for copy in out_local:
        copy.wait()
    for copy in out_sends:
        copy.wait()


def solution(mesh):
    nc = mesh.shape["ctx"] // 2
    nx = mesh.shape["head"]
    part = 512 // nc

    def body(query_rows, key_rows, value_rows, log_decay, step_size, band_mask, cotangent):
        tok, width = query_rows.shape
        out = jax.ShapeDtypeStruct((tok, width), BF16)
        hbm = pl.BlockSpec(memory_space=pl.ANY)
        vmem = pl.BlockSpec(memory_space=pltpu.VMEM)
        band = pltpu.VMEM((3, 2, D, HW), BF16)
        tile2 = pltpu.VMEM((2, 8, D), F32)
        share = pltpu.VMEM((nc, part, D), BF16)
        whole = pltpu.VMEM((HW, D), BF16)
        per_head = pltpu.VMEM((HH, T2, D), F32)
        square = pltpu.VMEM((HH, T2, T2), F32)
        return pl.pallas_call(
            functools.partial(kernel, nc, nx),
            name="mixer",
            out_shape=(out,) * 4,
            in_specs=[hbm] * 4 + [vmem] * 3,
            out_specs=(hbm,) * 4,
            scratch_shapes=[
                band, band, band, band, tile2, tile2, tile2,
                pltpu.VMEM((8, D), F32), pltpu.VMEM((nc, 8, D), F32),
                whole, share, share, whole,
                share, whole, share, whole,
                pltpu.VMEM((2 * nx, 8, T2), F32), pltpu.VMEM((3, 24, T2), F32),
                pltpu.VMEM((16, T2), F32), pltpu.VMEM((T2, 16), F32),
                pltpu.VMEM((8, W3), F32), pltpu.VMEM((8, W3), F32),
                square, square, pltpu.VMEM((HH, T2, T2), BF16),
                per_head, pltpu.VMEM((HH, T2, D), BF16),
                per_head, per_head, per_head, per_head,
                pltpu.VMEM((4, 2, D, HW), BF16),
                pltpu.SemaphoreType.DMA((48,)), pltpu.SemaphoreType.DMA((48,)),
                pltpu.SemaphoreType.DMA((8,)),
            ],
            compiler_params=pltpu.CompilerParams(
                collective_id=0, has_side_effects=True, vmem_limit_bytes=48 << 20
            ),
        )(query_rows, key_rows, value_rows, cotangent, log_decay, step_size, band_mask)

    return jax.shard_map(
        body,
        mesh=mesh,
        in_specs=(
            P("ctx", "head"),
            P("ctx", "head"),
            P("ctx", "head"),
            P("head", "ctx"),
            P("head", "ctx"),
            P("ctx", None),
            P("ctx", "head"),
        ),
        out_specs=(P("ctx", "head"), P("ctx", "head"), P("ctx", "head"), P("ctx", "head")),
        check_vma=False,
    )
```

time: 593 us -> 79.2 us (0.13)
  waiting for transfers between devices: 194 us -> 0 us
  blocking collectives: 171 us -> 0 us
  other arithmetic: 84.4 us -> 0 us
  Pallas kernels: 0 us -> 69.6 us
  matrix products: 58.2 us -> 0 us
  local copies, waits for them, and re-layouts: 38.6 us -> 8.63 us
  starting transfers between devices: 25.2 us -> 0 us
  between operations: 15.2 us -> 0.66 us
    all_gather x2 -> x0, waiting for transfers between devices: 159 us -> none  [prefix_2(): gathered = jax.tree.map(lambda a: lax.all_gather(a, axis), part)]
    unnamed x1 -> x0, blocking collectives: 156 us -> none
    add x64 -> x0, other arithmetic: 77.3 us -> none  [the longest x63 75.1 us: chain_states(): later[0][:, None, None] * earlier[1] + later[1]]
    pallas_call x0 -> x1, Pallas kernels: none -> 69.6 us  [body(): pl.pallas_call(functools.partial(kernel, nc, nx), name='mixer', out_shape...]
    dot_general x60 -> x0, matrix products: 58.2 us -> none  [the longest x8 9.74 us: per_head(): jnp.einsum('tu,ud->td', weights_bf, value_one, preferred_element_type=jnp...]
    ppermute x8 -> x0, waiting for transfers between devices: 35.1 us -> none  [passed_along(): return lax.ppermute(block, axis, route)]
    ppermute x8 -> x0, starting transfers between devices: 25.1 us -> none  [passed_along(): return lax.ppermute(block, axis, route)]
    psum x2 -> x0, blocking collectives: 14.7 us -> none  [the longest x1 8.48 us: body(): total_sq = lax.psum(squares, 'head')]
  transfers between devices with their start and end apart: 10 -> 0, of which waited for: 5 -> 0; matrix products, arithmetic and copies ran while one was open for 15% -> 0% of each run, Pallas kernels for 0% -> 0%
where the time goes in v1:
time: 79.2 us; the launch traced here: 78.9 us
  Pallas kernels  69.6 us (88%)
  local copies, waits for them, and re-layouts  8.63 us (11%)
    pallas_call x1, Pallas kernels, body(): pl.pallas_call(functools.partial(kernel, nc, nx), name='mixer', out_shape...  69.6 us
    unnamed x18, local copies, waits for them, and re-layouts  8.63 us

profile of v1, /device:TPU:1, one launch (start us, length us, event | category | flops | bytes accessed | tf_op | source)
XLA Modules:
  0.0 78.9 jit_solution(5322717878775101170)
XLA Ops:
  0.6 0.0 copy-start
  0.6 0.9 %copy-done = bf16[128,1024]{1,0:T(8,128)(2,1)S(1)} copy-done((bf16[128,1024]{1,0:T(8,128)(2,1)S(1)}, bf16[128,1024]{1,0:T(8,128)(2,1)}, u32[]{:S(2)}) %copy-start) | copy-done | bytes 262168
  1.6 0.0 copy-start.1
  1.6 0.9 %copy-done.1 = bf16[128,1024]{1,0:T(8,128)(2,1)S(1)} copy-done((bf16[128,1024]{1,0:T(8,128)(2,1)S(1)}, bf16[128,1024]{1,0:T(8,128)(2,1)}, u32[]{:S(2)}) %copy-start.1) | copy-done | bytes 262168
  2.5 0.0 copy-start.2
  2.5 0.9 %copy-done.2 = bf16[128,1024]{1,0:T(8,128)(2,1)S(1)} copy-done((bf16[128,1024]{1,0:T(8,128)(2,1)S(1)}, bf16[128,1024]{1,0:T(8,128)(2,1)}, u32[]{:S(2)}) %copy-start.2) | copy-done | bytes 262168
  3.5 0.0 copy-start.3
  3.5 0.9 %copy-done.3 = bf16[128,1024]{1,0:T(8,128)(2,1)S(1)} copy-done((bf16[128,1024]{1,0:T(8,128)(2,1)S(1)}, bf16[128,1024]{1,0:T(8,128)(2,1)}, u32[]{:S(2)}) %copy-start.3) | copy-done | bytes 262168
  4.4 0.0 copy-start.4
  4.4 0.7 copy-done.4
  5.1 0.0 copy-start.5
  5.1 0.7 copy-done.5
  5.8 0.0 copy-start.6
  5.8 0.7 copy-done.6
  6.5 69.6 %mixer.1 = (bf16[128,1024]{1,0:T(8,128)(2,1)S(1)}, bf16[128,1024]{1,0:T(8,128)(2,1)S(1)}, bf16[128,1024]{1,0:T(8,128)(2,1)S(1)}, bf16[128,1024]{1,0:T(8,128)(2,1)S(1)}) custom-call(bf16[128,1024]{1,0:T(8,128)(2,1)S(1)} %copy-done, bf16[128,1024]{1,0:T(8,128)(2,1)S(1)} %copy-done.1, bf16[128,1024]{1,0:T(8,128)(2,1)S(1)} %copy-done.2, ...), custom_call_target="tpu_custom_call" | custom-call | tf_op jit(solution)/shard_map/mixer/pallas_call | solution.py:442
  76.1 0.7 copy.15
  76.8 0.7 copy.16
  77.5 0.7 copy.17
  78.2 0.7 copy.18
Async XLA Ops:
  0.6 1.0 %copy-start = (bf16[128,1024]{1,0:T(8,128)(2,1)S(1)}, bf16[128,1024]{1,0:T(8,128)(2,1)}, u32[]{:S(2)}) copy-start(bf16[128,1024]{1,0:T(8,128)(2,1)} %q_ref.1) | copy-start | bytes 786436
  1.6 0.9 %copy-start.1 = (bf16[128,1024]{1,0:T(8,128)(2,1)S(1)}, bf16[128,1024]{1,0:T(8,128)(2,1)}, u32[]{:S(2)}) copy-start(bf16[128,1024]{1,0:T(8,128)(2,1)} %k_ref.1) | copy-start | bytes 786436
  2.5 0.9 %copy-start.2 = (bf16[128,1024]{1,0:T(8,128)(2,1)S(1)}, bf16[128,1024]{1,0:T(8,128)(2,1)}, u32[]{:S(2)}) copy-start(bf16[128,1024]{1,0:T(8,128)(2,1)} %v_ref.1) | copy-start | bytes 786436
  3.5 0.9 %copy-start.3 = (bf16[128,1024]{1,0:T(8,128)(2,1)S(1)}, bf16[128,1024]{1,0:T(8,128)(2,1)}, u32[]{:S(2)}) copy-start(bf16[128,1024]{1,0:T(8,128)(2,1)} %g_ref.1) | copy-start | bytes 786436
  4.4 0.7 copy-start.4
  5.1 0.7 copy-start.5
  5.8 0.7 copy-start.6

commit v2 on v1

v2 whole, which is shorter than its diff:
```python
import functools

import jax
import jax.numpy as jnp
from jax import lax
from jax.experimental import pallas as pl
from jax.experimental.pallas import tpu as pltpu
from jax.sharding import PartitionSpec as P

MESH = pl.DeviceIdType.MESH
HIGHEST = lax.Precision.HIGHEST
F32 = jnp.float32
BF16 = jnp.bfloat16
D = 128
HH = 4
HW = HH * D
T2 = 256
W3 = 768
CHANNELS = 4096
SCALE = D ** (-0.5)
BIG = 1e30
PLAN = {
    "p": ("k1a", "q1a"),
    "l": ("k1b", "q1b", "v1a", "g1a", "intra"),
    "e": ("v1b", "g1b", "k2a", "q2a", "k2b", "q2b"),
    "x": ("v2a", "g2a"),
    "o": ("v2b", "g2b", "soft", "ssd"),
    "b": ("query", "early", "late"),
}


def nn(a, b):
    return lax.dot_general(a, b, (((1,), (0,)), ((), ())), preferred_element_type=F32)


def nt(a, b):
    return lax.dot_general(a, b, (((1,), (1,)), ((), ())), preferred_element_type=F32)


def tn(a, b):
    return lax.dot_general(a, b, (((0,), (0,)), ((), ())), preferred_element_type=F32)


def kernel(
    nc, nx,
    q_ref, k_ref, v_ref, g_ref, ld_ref, st_ref, bm_ref,
    om_ref, oq_ref, ok_ref, ov_ref,
    kb, vb, qb, gb, kx, vx, ldb, stb, mk, bmv, part_out, part_in, f_in, l_out, l_in, e_out, e_in,
    o_in, o_out, b_out, b_in, xs, stat, rows, cols, bias, big,
    mix, mixt, pairt, qt, ssd, dss, wq, wk, dq, dk, dv, outs,
    ssem, rsem, lsem,
):
    me = lax.axis_index("ctx")
    x = lax.axis_index("head")
    c = me // 2
    j = me % 2
    part = 512 // nc

    def dev(chip, core, xx):
        return (lax.rem(chip, nc) * 2 + core, xx)

    def order(n):
        half = (n + 1) // 2
        return nc // 2 + jnp.where(n % 2 == 0, half, -half)

    barrier = pltpu.get_barrier_semaphore()

    def greet(n, carry):
        pl.semaphore_signal(barrier, 1, device_id=dev(c + order(n), j, x), device_id_type=MESH)
        return carry

    lax.fori_loop(0, nc - 1, greet, 0)
    greeted = nc - 1
    for other in (dev(c + 1, 1 - j, x), dev(c + nc - 1, 1 - j, x), dev(c, 1 - j, x)):
        pl.semaphore_signal(barrier, 1, device_id=other, device_id_type=MESH)
        greeted += 1
    for step in range(1, nx):
        for core in range(2):
            pl.semaphore_signal(
                barrier, 1, device_id=dev(c, core, lax.rem(x + step, nx)), device_id_type=MESH
            )
            greeted += 1

    sends = []
    count = {"s": 0, "r": 0}

    def slots(kind, n):
        at = count[kind]
        count[kind] += n
        return at

    def remote(src, dst, recv, target):
        copy = pltpu.make_async_remote_copy(
            src_ref=src, dst_ref=dst, send_sem=ssem.at[slots("s", 1)], recv_sem=rsem.at[recv],
            device_id=target, device_id_type=MESH,
        )
        sends.append((copy, src))
        copy.start()

    def arrived(ref, recv):
        pltpu.make_async_copy(ref, ref, rsem.at[recv]).wait()

    mine = pl.ds(pl.multiple_of(j * HW, HW), HW)
    other_half = pl.ds(pl.multiple_of((1 - j) * HW, HW), HW)
    local = []
    for n, (src, dst) in enumerate(
        (
            (ld_ref, ldb.at[j]), (st_ref, stb.at[j]), (bm_ref, bmv),
            (k_ref.at[:, mine], kb.at[2, j]), (v_ref.at[:, mine], vb.at[2, j]),
            (k_ref.at[:, other_half], kx), (v_ref.at[:, other_half], vx),
            (q_ref.at[:, mine], qb.at[0, j]), (g_ref.at[:, mine], gb.at[0, j]),
        )
    ):
        copy = pltpu.make_async_copy(src, dst, lsem.at[n])
        copy.start()
        local.append(copy)
    low = j == 0
    at_row = lax.broadcasted_iota(jnp.int32, (T2, T2), 0)
    at_col = lax.broadcasted_iota(jnp.int32, (T2, T2), 1)
    upper = (at_row <= at_col).astype(F32)
    for copy in local[0:3]:
        copy.wait()
    listed = bmv[...].astype(F32)
    mk[j] = jnp.concatenate(
        [jnp.broadcast_to(listed[:, n : n + 1], (1, D)) for n in range(5)]
        + [jnp.zeros((3, D), F32)],
        axis=0,
    )
    own_prefix = lax.dot_general(
        ldb[j], upper[0:D, 0:D], (((1,), (0,)), ((), ())),
        precision=HIGHEST, preferred_element_type=F32,
    )
    own_carry = jnp.transpose(jnp.exp(own_prefix[:, D - 1 : D] - own_prefix) * stb[j])
    carry_mine = jnp.where(low, own_carry[:, 0:HH], own_carry[:, HH : 2 * HH])
    carry_mate = jnp.where(low, own_carry[:, HH : 2 * HH], own_carry[:, 0:HH])
    for copy in local[3:7]:
        copy.wait()
    for h in range(HH):
        cut = slice(h * D, (h + 1) * D)
        part_out[cut, :] = tn(
            (carry_mate[:, h : h + 1] * kx[:, cut].astype(F32)).astype(BF16), vx[:, cut]
        )
        part_in[j, cut, :] = tn(
            (carry_mine[:, h : h + 1] * kb[2, j, :, cut].astype(F32)).astype(BF16),
            vb[2, j, :, cut],
        )

    pl.semaphore_wait(barrier, greeted)

    mate = dev(c, 1 - j, x)
    small = slots("r", 4)
    remote(ldb.at[j], ldb.at[j], small, mate)
    remote(stb.at[j], stb.at[j], small + 1, mate)
    remote(part_out, part_in.at[j], small + 2, mate)
    remote(mk.at[j], mk.at[j], small + 3, mate)
    swap = slots("r", 4)

    def swap_send(n, src, dst, slot):
        remote(src, dst.at[slot, j], swap + n, mate)

    swap_send(0, kx, kb, 2)
    swap_send(1, vx, vb, 2)
    swap_send(2, q_ref.at[:, other_half], qb, 0)
    swap_send(3, g_ref.at[:, other_half], gb, 0)

    first = slots("r", 16)
    second = slots("r", 16)
    ways = {
        "k": (0, k_ref, kb, 0, 1), "q": (1, q_ref, qb, 2, nc - 1),
        "v": (2, v_ref, vb, 0, 1), "g": (3, g_ref, gb, 2, nc - 1),
    }

    def half(name):
        at = 4 * ways[name[0]][0] + 2 * (name[2] == "b")
        return pl.ds(64 * (name[2] == "b"), 64), first + at, second + at

    def own_on(name):
        _, src, dst, _, step = ways[name[0]]
        lines, near, _ = half(name)
        for core in range(2):
            remote(
                src.at[lines, pl.ds(core * HW, HW)], dst.at[1, j, lines], near + j,
                dev(c + step, core, x),
            )

    def hand_on(name):
        _, _, buf, far, step = ways[name[0]]
        lines, near, later = half(name)
        for core in range(2):
            arrived(buf.at[1, core, lines], near + core)
            remote(
                buf.at[1, core, lines], buf.at[far, core, lines], later + core, dev(c + step, j, x)
            )

    def landed(name):
        _, _, buf, far, _ = ways[name]
        for end in "ab":
            lines, _, later = half(name + "2" + end)
            for core in range(2):
                arrived(buf.at[far, core, lines], later + core)

    acts = {}

    def during(window):
        for item in PLAN[window]:
            if item in acts:
                acts[item]()
            elif item[1] == "1":
                own_on(item)
            else:
                hand_on(item)

    during("p")

    arrived(ldb.at[1 - j], small)
    arrived(stb.at[1 - j], small + 1)
    pair = []
    for ref in (ldb, stb):
        wide = jnp.concatenate([ref[0], ref[1]], axis=1)
        pair.append(jnp.where(low, wide[0:HH], wide[HH : 2 * HH]))
    decay, step_row = pair
    last_wide = jnp.broadcast_to(jnp.sum(decay, axis=1, keepdims=True), (HH, D))
    f_in[pl.ds(c, 1)] = jnp.concatenate([last_wide, last_wide], axis=0)[None]

    def exchange(src_of, dst_of):
        s_at, r_at = slots("s", 1), slots("r", 1)

        def one(n, carry):
            chip = lax.rem(c + order(n), nc)
            pltpu.make_async_remote_copy(
                src_ref=src_of(chip), dst_ref=dst_of(c), send_sem=ssem.at[s_at],
                recv_sem=rsem.at[r_at], device_id=(chip * 2 + j, x), device_id_type=MESH,
            ).start()
            return carry

        lax.fori_loop(0, nc - 1, one, 0)
        return s_at, r_at

    def own(chip):
        return pl.ds(pl.multiple_of(chip * part, part), part)

    def head(ref, slot, h):
        return ref[slot, :, :, h * D : (h + 1) * D].reshape(T2, D)

    def band(ref, h):
        return ref[:, :, :, h * D : (h + 1) * D].reshape(W3, D)

    fade_late = jnp.exp(jnp.sum(decay[:, D : 2 * D], axis=1, keepdims=True))
    arrived(part_in.at[1 - j], small + 2)
    for h in range(HH):
        cut = slice(h * D, (h + 1) * D)
        l_out[cut, :] = (fade_late[h : h + 1, :] * part_in[0, cut, :] + part_in[1, cut, :]).astype(BF16)
    l_sem = exchange(lambda chip: l_out.at[own(chip)], lambda sender: l_in.at[sender])
    l_in[pl.ds(c, 1)] = l_out[own(c), :][None]

    f_sem = exchange(lambda chip: f_in.at[c], lambda sender: f_in.at[sender])

    blank = jnp.full((1, D), BIG, F32)

    def intra():
        prefix = lax.dot_general(
            jnp.concatenate([decay, decay], axis=0), upper, (((1,), (0,)), ((), ())),
            precision=HIGHEST, preferred_element_type=F32,
        )[0:HH]
        last = prefix[:, T2 - 1 : T2]
        carry_row = jnp.exp(last - prefix) * step_row
        packed = jnp.concatenate([prefix, step_row, carry_row, jnp.exp(prefix)], axis=0)
        rows[...] = packed
        cols[...] = jnp.transpose(packed)

        arrived(mk.at[1 - j], small + 3)

        for core in range(2):
            line = []
            for dist in (2, 1, 0):
                for core_k in range(2):
                    off = 2 * dist + core - core_k
                    line.append((1.0 - mk[core, off : off + 1, :]) * BIG if 0 <= off < 5 else blank)
            bias[core : core + 1, :] = jnp.concatenate(line, axis=1) * -1.0

        for copy in local[7:9]:
            copy.wait()
        arrived(kb.at[2, 1 - j], swap)
        arrived(vb.at[2, 1 - j], swap + 1)
        arrived(qb.at[0, 1 - j], swap + 2)
        arrived(gb.at[0, 1 - j], swap + 3)
        for h in range(HH):
            q, k, v = head(qb, 0, h), head(kb, 2, h), head(vb, 2, h)
            p_row, p_col = rows[h : h + 1, :], cols[:, h : h + 1]
            m = jnp.exp(jnp.where(at_row >= at_col, p_col - p_row, -BIG)) * (
                rows[4 + h : 5 + h, :] * SCALE
            )
            mix[h] = m
            ssd[h] = nn((m * nt(q, k)).astype(BF16), v)
            mt = jnp.exp(jnp.where(at_row <= at_col, p_row - p_col, -BIG)) * (
                cols[:, 4 + h : 5 + h] * SCALE
            )
            mixt[h] = mt
            pairt[h] = (mt * nt(k, q)).astype(BF16)
            qt[h] = jnp.transpose(cols[:, 12 + h : 13 + h] * q.astype(F32)).astype(BF16)

    acts["intra"] = intra
    during("l")

    def total(ref):
        return ref.at[pl.ds(0, nc - 1)]

    head_of = c * part // D
    arrived(total(f_in), f_sem[1])
    arrived(total(l_in), l_sem[1])

    def scan(src, dst, reverse):
        def one(n, run):
            chip = nc - 1 - n if reverse else n
            dst[pl.ds(chip, 1)] = run.astype(BF16)[None]
            fade = jnp.exp(f_in[pl.ds(chip, 1), pl.ds(head_of, 1), :][0])
            return fade * run + src[pl.ds(chip, 1)][0].astype(F32)

        lax.fori_loop(0, nc, one, jnp.zeros((part, D), F32), unroll=True)

    scan(l_in, e_out, False)
    e_sem = exchange(lambda chip: e_out.at[chip], lambda sender: e_in.at[own(sender)])
    e_in[own(c), :] = e_out[pl.ds(c, 1)][0]

    during("e")

    rest = e_in.at[pl.ds(0, 512 - part)]
    arrived(rest, e_sem[1])
    squares = jnp.zeros((T2, D), F32)
    inner = jnp.zeros((T2, D), F32)
    for h in range(HH):
        state = e_in[h * D : (h + 1) * D, :]
        y = ssd[h] + (SCALE * cols[:, 12 + h : 13 + h]) * nn(head(qb, 0, h), state)
        ssd[h] = y
        squares = squares + y * y
        inner = inner + y * head(gb, 0, h).astype(F32)
    ones = jnp.ones((8, D), BF16)

    def across(a):
        head_part = a.astype(BF16)
        return nt(ones, head_part) + nt(ones, (a - head_part.astype(F32)).astype(BF16))

    sums = jnp.concatenate([across(squares)[0:4], across(inner)[0:4]], axis=0)
    here = x * 2 + j
    xs[pl.ds(here, 1)] = sums[None]
    x_s, x_r = slots("s", 1), slots("r", 1)
    for step in range(nx):
        for core in range(2):
            if step == 0 and core == 0:
                continue
            pltpu.make_async_remote_copy(
                src_ref=xs.at[here], dst_ref=xs.at[here], send_sem=ssem.at[x_s],
                recv_sem=rsem.at[x_r],
                device_id=dev(c, (j + core) % 2, lax.rem(x + step, nx)), device_id_type=MESH,
            ).start()

    columns = []

    def turned_rows(kinds):
        lane = lax.broadcasted_iota(jnp.int32, (T2, D), 1)
        grid = jnp.zeros((T2, D), F32)
        for n, column in enumerate(kinds):
            grid = jnp.where(lane == n, column, grid)
        return jnp.transpose(grid)[0:8]

    def send_stat(lines, at):
        for dist in (1, 2):
            remote(
                stat.at[0, lines], stat.at[dist, lines], at + dist - 1, dev(c + nc - dist, j, x)
            )

    stat_r = slots("r", 4)

    def soft():
        landed("k")
        for h in range(HH):
            s = nt(head(qb, 0, h), band(kb, h)) * SCALE
            s = (s.reshape(2, D, W3) + bias[0:2, :][:, None, :]).reshape(T2, W3)
            peak = jnp.max(s, axis=-1, keepdims=True)
            e = jnp.exp(s - peak)
            inv = 1.0 / jnp.sum(e, axis=-1, keepdims=True)
            wq[h] = e * inv
            columns.append((peak, inv))
        stat[0, 0:8, :] = turned_rows([p for p, _ in columns] + [i for _, i in columns])
        stat[0, 8:16, :] = jnp.concatenate([mk[0], mk[1]], axis=1)
        send_stat(pl.ds(0, 16), stat_r)

    acts["soft"] = soft
    during("x")

    arrived(xs.at[pl.ds(0, 2 * nx - 1)], x_r)
    both = xs[0]
    for n in range(1, 2 * nx):
        both = both + xs[n]
    inv_root = 1.0 / jnp.sqrt(both[0:4] / CHANNELS + 1e-05)
    cross = both[4:8] * inv_root / CHANNELS
    turned = jnp.transpose(jnp.concatenate([inv_root, inv_root * inv_root * cross], axis=0))
    root_col, slope_col = turned[:, 0:1], turned[:, 4:5]
    for h in range(HH):
        g = head(gb, 0, h).astype(F32)
        y = ssd[h]
        d = (g * root_col - y * slope_col).astype(BF16)
        dss[h] = d
        o_out[h * D : (h + 1) * D, :] = (SCALE * nn(qt[h], d)).astype(BF16)
    o_in[pl.ds(c, 1)] = o_out[own(c), :][None]
    o_sem = exchange(lambda chip: o_out.at[own(chip)], lambda sender: o_in.at[sender])

    out_sends = []
    out_local = []
    out_r = slots("r", 4)

    def emit(n, ref):
        copy = pltpu.make_async_copy(outs.at[n, j], ref.at[:, mine], lsem.at[9 + n])
        copy.start()
        out_local.append(copy)
        far = pltpu.make_async_remote_copy(
            src_ref=outs.at[n, 1 - j], dst_ref=ref.at[:, mine], send_sem=ssem.at[slots("s", 1)],
            recv_sem=rsem.at[out_r + n], device_id=mate, device_id_type=MESH,
        )
        far.start()
        out_sends.append(far)

    def put(n, h, value):
        outs[n, :, :, h * D : (h + 1) * D] = value.astype(BF16).reshape(2, D, D)

    def ssd_grads():
        for h in range(HH):
            q, k, v, d = head(qb, 0, h), head(kb, 2, h), head(vb, 2, h), dss[h]
            state = e_in[h * D : (h + 1) * D, :]
            grad = nn((mix[h] * nt(d, v)).astype(BF16), k)
            grad = grad + (SCALE * cols[:, 12 + h : 13 + h]) * nt(d, state)
            dq[h] = grad
            dk[h] = nn((mixt[h] * nt(v, d)).astype(BF16), q)
            dv[h] = nn(pairt[h], d)

    acts["ssd"] = ssd_grads
    during("o")

    arrived(total(o_in), o_sem[1])
    scan(o_in, b_out, True)
    b_sem = exchange(lambda chip: b_out.at[chip], lambda sender: b_in.at[own(sender)])
    b_in[own(c), :] = b_out[pl.ds(c, 1)][0]

    def query():
        landed("v")
        inners = []
        for h in range(HH):
            g, k, v, w = head(gb, 0, h), band(kb, h), band(vb, h), wq[h]
            a = nn(w.astype(BF16), v)
            row_inner = jnp.sum(g.astype(F32) * a, axis=-1, keepdims=True)
            inners.append(row_inner)
            put(0, h, a + ssd[h] * root_col)
            gs = (SCALE * w * (nt(g, v) - row_inner)).astype(BF16)
            put(1, h, nn(gs, k) + dq[h])
        stat[0, 16:24, :] = turned_rows(inners)
        send_stat(pl.ds(16, 8), stat_r + 2)
        emit(0, om_ref)
        emit(1, oq_ref)

    def early():
        for dist in (1, 2):
            arrived(stat.at[dist, pl.ds(0, 16)], stat_r + dist - 1)
        landed("q")
        for core_k in range(2):
            line = []
            for dist in range(3):
                here_ok = c + dist < nc
                for core in range(2):
                    off = 2 * dist + core - core_k
                    if 0 <= off < 5:
                        listed = stat[dist, 8 + off : 9 + off, core * D : (core + 1) * D]
                        line.append(jnp.where(here_ok, (1.0 - listed) * BIG, BIG))
                    else:
                        line.append(blank)
            big[core_k : core_k + 1, :] = jnp.concatenate(line, axis=1)
        landed("g")
        for h in range(HH):
            q, g, k = band(qb, h), band(gb, h), head(kb, 2, h)
            peak, inv = [
                jnp.concatenate([stat[n, at : at + 1, :] for n in range(3)], axis=1)
                for at in (h, HH + h)
            ]
            shift = peak + big[0:2, :]
            s = nt(k, q) * SCALE
            w = jnp.exp((s.reshape(2, D, W3) - shift[:, None, :]).reshape(T2, W3)) * inv
            dv[h] = dv[h] + nn(w.astype(BF16), g)
            wk[h] = w

    def late():
        for dist in (1, 2):
            arrived(stat.at[dist, pl.ds(16, 8)], stat_r + 1 + dist)
        for h in range(HH):
            row_inner = jnp.concatenate([stat[n, 16 + h : 17 + h, :] for n in range(3)], axis=1)
            gs = (SCALE * wk[h] * (nt(head(vb, 2, h), band(gb, h)) - row_inner)).astype(BF16)
            dk[h] = dk[h] + nn(gs, band(qb, h))

    acts["query"], acts["early"], acts["late"] = query, early, late
    during("b")

    arrived(b_in.at[pl.ds(0, 512 - part)], b_sem[1])
    for h in range(HH):
        state = b_in[h * D : (h + 1) * D, :]
        weight = cols[:, 8 + h : 9 + h]
        put(2, h, dk[h] + weight * nt(head(vb, 2, h), state))
    emit(2, ok_ref)
    for h in range(HH):
        state = b_in[h * D : (h + 1) * D, :]
        weight = cols[:, 8 + h : 9 + h]
        put(3, h, dv[h] + weight * nn(head(kb, 2, h), state))
    emit(3, ov_ref)

    for copy, _ in sends:
        copy.wait_send()
    pltpu.make_async_copy(total(f_in), total(f_in), ssem.at[f_sem[0]]).wait()
    for ref, sem in ((l_in, l_sem), (e_out, e_sem), (o_in, o_sem), (b_out, b_sem)):
        pltpu.make_async_copy(total(ref), total(ref), ssem.at[sem[0]]).wait()
    rest_x = xs.at[pl.ds(0, 2 * nx - 1)]
    pltpu.make_async_copy(rest_x, rest_x, ssem.at[x_s]).wait()
    for copy in out_local:
        copy.wait()
    for copy in out_sends:
        copy.wait()


def store(a, b, c, d, ra, rb, rc, rd):
    for src, dst in ((a, ra), (b, rb), (c, rc), (d, rd)):
        dst[...] = src[...]


def solution(mesh):
    nc = mesh.shape["ctx"] // 2
    nx = mesh.shape["head"]
    part = 512 // nc

    def body(query_rows, key_rows, value_rows, log_decay, step_size, band_mask, cotangent):
        tok, width = query_rows.shape
        out = jax.ShapeDtypeStruct((tok, width), BF16)
        hbm = pl.BlockSpec(memory_space=pltpu.HBM)
        band = pltpu.VMEM((3, 2, D, HW), BF16)
        tile2 = pltpu.VMEM((2, 8, D), F32)
        share = pltpu.VMEM((nc, part, D), BF16)
        whole = pltpu.VMEM((HW, D), BF16)
        per_head = pltpu.VMEM((HH, T2, D), F32)
        square = pltpu.VMEM((HH, T2, T2), F32)
        results = pl.pallas_call(
            functools.partial(kernel, nc, nx),
            name="mixer",
            out_shape=(out,) * 4,
            in_specs=[hbm] * 7,
            out_specs=(pl.BlockSpec(memory_space=pl.ANY),) * 4,
            scratch_shapes=[
                band, band, band, band, pltpu.VMEM((D, HW), BF16), pltpu.VMEM((D, HW), BF16),
                tile2, tile2, tile2, pltpu.VMEM((1, 5), jnp.int32),
                pltpu.VMEM((HW, D), F32), pltpu.VMEM((2, HW, D), F32), pltpu.VMEM((nc, 8, D), F32),
                whole, share, share, whole,
                share, whole, share, whole,
                pltpu.VMEM((2 * nx, 8, T2), F32), pltpu.VMEM((3, 24, T2), F32),
                pltpu.VMEM((16, T2), F32), pltpu.VMEM((T2, 16), F32),
                pltpu.VMEM((8, W3), F32), pltpu.VMEM((8, W3), F32),
                square, square, pltpu.VMEM((HH, T2, T2), BF16), pltpu.VMEM((HH, D, T2), BF16),
                per_head, pltpu.VMEM((HH, T2, D), BF16),
                pltpu.VMEM((HH, T2, W3), F32), pltpu.VMEM((HH, T2, W3), F32),
                per_head, per_head, per_head,
                pltpu.VMEM((4, 2, D, HW), BF16),
                pltpu.SemaphoreType.DMA((80,)), pltpu.SemaphoreType.DMA((80,)),
                pltpu.SemaphoreType.DMA((16,)),
            ],
            compiler_params=pltpu.CompilerParams(
                collective_id=0, has_side_effects=True, vmem_limit_bytes=56 << 20
            ),
        )(query_rows, key_rows, value_rows, cotangent, log_decay, step_size, band_mask)
        return pl.pallas_call(
            store,
            name="store",
            out_shape=(out,) * 4,
            grid=(2,),
            in_specs=[pl.BlockSpec((tok // 2, width), lambda n: (n, 0))] * 4,
            out_specs=(pl.BlockSpec((tok // 2, width), lambda n: (n, 0)),) * 4,
        )(*results)

    return jax.shard_map(
        body,
        mesh=mesh,
        in_specs=(
            P("ctx", "head"),
            P("ctx", "head"),
            P("ctx", "head"),
            P("head", "ctx"),
            P("head", "ctx"),
            P("ctx", None),
            P("ctx", "head"),
        ),
        out_specs=(P("ctx", "head"), P("ctx", "head"), P("ctx", "head"), P("ctx", "head")),
        check_vma=False,
    )
```

time: 79.2 us -> 59.4 us (0.75)
  Pallas kernels: 69.6 us -> 58.6 us
  local copies, waits for them, and re-layouts: 8.63 us -> 0 us
    pallas_call x1, Pallas kernels: 69.6 us -> 56.5 us  [body(): pl.pallas_call(functools.partial(kernel, nc, nx), name='mixer', out_shape...]
    unnamed x18 -> x0, local copies, waits for them, and re-layouts: 8.63 us -> none
    pallas_call x0 -> x1, Pallas kernels: none -> 2.13 us  [body(): pl.pallas_call(store, name='store', out_shape=(out,) * 4, grid=(2,), in_s...]
where the time goes in v2:
time: 59.4 us; the launch traced here: 59.3 us
  Pallas kernels  58.6 us (99%)
  between operations  0.64 us (1%)
    pallas_call x1, Pallas kernels, body(): pl.pallas_call(functools.partial(kernel, nc, nx), name='mixer', out_shape...  56.5 us
    pallas_call x1, Pallas kernels, body(): pl.pallas_call(store, name='store', out_shape=(out,) * 4, grid=(2,), in_s...  2.13 us

profile of v2, /device:TPU:1, one launch (start us, length us, event | category | flops | bytes accessed | tf_op | source)
XLA Modules:
  0.0 59.3 jit_solution(7640708870964634005)
XLA Ops:
  0.6 56.5 %mixer.1 = (bf16[128,1024]{1,0:T(8,128)(2,1)}, bf16[128,1024]{1,0:T(8,128)(2,1)}, bf16[128,1024]{1,0:T(8,128)(2,1)}, bf16[128,1024]{1,0:T(8,128)(2,1)}) custom-call(bf16[128,1024]{1,0:T(8,128)(2,1)} %q_ref.1, bf16[128,1024]{1,0:T(8,128)(2,1)} %k_ref.1, bf16[128,1024]{1,0:T(8,128)(2,1)} %v_ref.1, bf16[128,1024]{1,0:T(8,128)(2,1)} %g_ref.1, f32[8,128]{1,0:T(8,128)} %ld_ref.1, ...), custom_call_target="tpu_custom_call" | custom-call | tf_op jit(solution)/shard_map/mixer/pallas_call | solution.py:545
  57.1 2.1 %store.1 = (bf16[128,1024]{1,0:T(8,128)(2,1)}, bf16[128,1024]{1,0:T(8,128)(2,1)}, bf16[128,1024]{1,0:T(8,128)(2,1)}, bf16[128,1024]{1,0:T(8,128)(2,1)}) custom-call(bf16[128,1024]{1,0:T(8,128)(2,1)} %get-tuple-element.8.a, bf16[128,1024]{1,0:T(8,128)(2,1)} %get-tuple-element.9.b, bf16[128,1024]{1,0:T(8,128)(2,1)} %get-tuple-element.10.c, ...), custom_call_target="tpu_custom_call" | custom-call | tf_op jit(solution)/shard_map/store/pallas_call | solution.py:572

commit v3 on v2

--- a/solution.py
+++ b/solution.py
@@ -233,7 +233,7 @@
             ).start()
             return carry
 
-        lax.fori_loop(0, nc - 1, one, 0)
+        lax.fori_loop(0, nc - 1, one, 0, unroll=True)
         return s_at, r_at
 
     def own(chip):
@@ -522,9 +522,15 @@
         copy.wait()
 
 
-def store(a, b, c, d, ra, rb, rc, rd):
-    for src, dst in ((a, ra), (b, rb), (c, rc), (d, rd)):
-        dst[...] = src[...]
+def store(a, b, c, d, ra, rb, rc, rd, sem):
+    copies = [
+        pltpu.make_async_copy(src, dst, sem.at[n])
+        for n, (src, dst) in enumerate(((a, ra), (b, rb), (c, rc), (d, rd)))
+    ]
+    for copy in copies:
+        copy.start()
+    for copy in copies:
+        copy.wait()
 
 
 def solution(mesh):
@@ -545,9 +551,9 @@
         results = pl.pallas_call(
             functools.partial(kernel, nc, nx),
             name="mixer",
-            out_shape=(out,) * 4,
+            out_shape=(pltpu.VMEM((tok, width), BF16),) * 4,
             in_specs=[hbm] * 7,
-            out_specs=(pl.BlockSpec(memory_space=pl.ANY),) * 4,
+            out_specs=(pl.BlockSpec(memory_space=pltpu.VMEM),) * 4,
             scratch_shapes=[
                 band, band, band, band, pltpu.VMEM((D, HW), BF16), pltpu.VMEM((D, HW), BF16),
                 tile2, tile2, tile2, pltpu.VMEM((1, 5), jnp.int32),
@@ -568,15 +574,22 @@
             compiler_params=pltpu.CompilerParams(
                 collective_id=0, has_side_effects=True, vmem_limit_bytes=56 << 20
             ),
-        )(query_rows, key_rows, value_rows, cotangent, log_decay, step_size, band_mask)
+        )(
+            *[
+                pltpu.with_memory_space_constraint(a, pltpu.HBM)
+                for a in (
+                    query_rows, key_rows, value_rows, cotangent, log_decay, step_size, band_mask
+                )
+            ]
+        )
         return pl.pallas_call(
             store,
             name="store",
             out_shape=(out,) * 4,
-            grid=(2,),
-            in_specs=[pl.BlockSpec((tok // 2, width), lambda n: (n, 0))] * 4,
-            out_specs=(pl.BlockSpec((tok // 2, width), lambda n: (n, 0)),) * 4,
-        )(*results)
+            in_specs=[pl.BlockSpec(memory_space=pltpu.VMEM)] * 4,
+            out_specs=(hbm,) * 4,
+            scratch_shapes=[pltpu.SemaphoreType.DMA((4,))],
+        )(*[pltpu.with_memory_space_constraint(a, pltpu.VMEM) for a in results])
 
     return jax.shard_map(
         body,

time: 59.4 us -> 58.8 us (0.990)
  Pallas kernels: 58.6 us -> 58 us
    pallas_call x1, Pallas kernels: 2.13 us -> 1 us  [body(): pl.pallas_call(store, name='store', out_shape=(out,) * 4, in_specs=[pl.Bl...]
where the time goes in v3:
time: 58.8 us; the launch traced here: 58.7 us
  Pallas kernels  58 us (99%)
  between operations  0.64 us (1%)
    pallas_call x1, Pallas kernels, body(): pl.pallas_call(functools.partial(kernel, nc, nx), name='mixer', out_shape...  57 us

profile of v3, /device:TPU:1, one launch (start us, length us, event | category | flops | bytes accessed | tf_op | source)
XLA Modules:
  0.0 58.7 jit_solution(11271808883764560647)
XLA Ops:
  0.6 57.0 %mixer.1 = (bf16[128,1024]{1,0:T(8,128)(2,1)S(1)}, bf16[128,1024]{1,0:T(8,128)(2,1)S(1)}, bf16[128,1024]{1,0:T(8,128)(2,1)S(1)}, bf16[128,1024]{1,0:T(8,128)(2,1)S(1)}) custom-call(bf16[128,1024]{1,0:T(8,128)(2,1)} %q_ref.1, bf16[128,1024]{1,0:T(8,128)(2,1)} %k_ref.1, bf16[128,1024]{1,0:T(8,128)(2,1)} %v_ref.1, bf16[128,1024]{1,0:T(8,128)(2,1)} %g_ref.1, ...), custom_call_target="tpu_custom_call" | custom-call | tf_op jit(solution)/shard_map/mixer/pallas_call | solution.py:551
  57.7 1.0 %store.1 = (bf16[128,1024]{1,0:T(8,128)(2,1)}, bf16[128,1024]{1,0:T(8,128)(2,1)}, bf16[128,1024]{1,0:T(8,128)(2,1)}, bf16[128,1024]{1,0:T(8,128)(2,1)}) custom-call(bf16[128,1024]{1,0:T(8,128)(2,1)S(1)} %get-tuple-element.8.a, bf16[128,1024]{1,0:T(8,128)(2,1)S(1)} %get-tuple-element.9.b, bf16[128,1024]{1,0:T(8,128)(2,1)S(1)} %get-tuple-element.10.c, ...), custom_call_target="tpu_custom_call" | custom-call | tf_op jit(solution)/shard_map/store/pallas_call | solution.py:585

commit v4 on v3

--- a/solution.py
+++ b/solution.py
@@ -99,6 +99,29 @@
 
     def arrived(ref, recv):
         pltpu.make_async_copy(ref, ref, rsem.at[recv]).wait()
+
+    def exchange(src_of, dst_of):
+        s_at, r_at = slots("s", 1), slots("r", 1)
+
+        def one(n, carry):
+            chip = lax.rem(c + order(n), nc)
+            pltpu.make_async_remote_copy(
+                src_ref=src_of(chip), dst_ref=dst_of(c), send_sem=ssem.at[s_at],
+                recv_sem=rsem.at[r_at], device_id=(chip * 2 + j, x), device_id_type=MESH,
+            ).start()
+            return carry
+
+        lax.fori_loop(0, nc - 1, one, 0, unroll=True)
+        return s_at, r_at
+
+    def own(chip):
+        return pl.ds(pl.multiple_of(chip * part, part), part)
+
+    def head(ref, slot, h):
+        return ref[slot, :, :, h * D : (h + 1) * D].reshape(T2, D)
+
+    def band(ref, h):
+        return ref[:, :, :, h * D : (h + 1) * D].reshape(W3, D)
 
     mine = pl.ds(pl.multiple_of(j * HW, HW), HW)
     other_half = pl.ds(pl.multiple_of((1 - j) * HW, HW), HW)
@@ -130,6 +153,8 @@
         ldb[j], upper[0:D, 0:D], (((1,), (0,)), ((), ())),
         precision=HIGHEST, preferred_element_type=F32,
     )
+    own_last = jnp.broadcast_to(own_prefix[:, D - 1 : D], (8, D))
+    f_in[pl.ds(j, 1), pl.ds(c, 1)] = own_last[None, None]
     own_carry = jnp.transpose(jnp.exp(own_prefix[:, D - 1 : D] - own_prefix) * stb[j])
     carry_mine = jnp.where(low, own_carry[:, 0:HH], own_carry[:, HH : 2 * HH])
     carry_mate = jnp.where(low, own_carry[:, HH : 2 * HH], own_carry[:, 0:HH])
@@ -153,6 +178,7 @@
     remote(stb.at[j], stb.at[j], small + 1, mate)
     remote(part_out, part_in.at[j], small + 2, mate)
     remote(mk.at[j], mk.at[j], small + 3, mate)
+    f_sem = exchange(lambda chip: f_in.at[j, c], lambda sender: f_in.at[j, sender])
     swap = slots("r", 4)
 
     def swap_send(n, src, dst, slot):
@@ -219,31 +245,6 @@
         wide = jnp.concatenate([ref[0], ref[1]], axis=1)
         pair.append(jnp.where(low, wide[0:HH], wide[HH : 2 * HH]))
     decay, step_row = pair
-    last_wide = jnp.broadcast_to(jnp.sum(decay, axis=1, keepdims=True), (HH, D))
-    f_in[pl.ds(c, 1)] = jnp.concatenate([last_wide, last_wide], axis=0)[None]
-
-    def exchange(src_of, dst_of):
-        s_at, r_at = slots("s", 1), slots("r", 1)
-
-        def one(n, carry):
-            chip = lax.rem(c + order(n), nc)
-            pltpu.make_async_remote_copy(
-                src_ref=src_of(chip), dst_ref=dst_of(c), send_sem=ssem.at[s_at],
-                recv_sem=rsem.at[r_at], device_id=(chip * 2 + j, x), device_id_type=MESH,
-            ).start()
-            return carry
-
-        lax.fori_loop(0, nc - 1, one, 0, unroll=True)
-        return s_at, r_at
-
-    def own(chip):
-        return pl.ds(pl.multiple_of(chip * part, part), part)
-
-    def head(ref, slot, h):
-        return ref[slot, :, :, h * D : (h + 1) * D].reshape(T2, D)
-
-    def band(ref, h):
-        return ref[:, :, :, h * D : (h + 1) * D].reshape(W3, D)
 
     fade_late = jnp.exp(jnp.sum(decay[:, D : 2 * D], axis=1, keepdims=True))
     arrived(part_in.at[1 - j], small + 2)
@@ -252,8 +253,6 @@
         l_out[cut, :] = (fade_late[h : h + 1, :] * part_in[0, cut, :] + part_in[1, cut, :]).astype(BF16)
     l_sem = exchange(lambda chip: l_out.at[own(chip)], lambda sender: l_in.at[sender])
     l_in[pl.ds(c, 1)] = l_out[own(c), :][None]
-
-    f_sem = exchange(lambda chip: f_in.at[c], lambda sender: f_in.at[sender])
 
     blank = jnp.full((1, D), BIG, F32)
 
@@ -305,15 +304,22 @@
     def total(ref):
         return ref.at[pl.ds(0, nc - 1)]
 
-    head_of = c * part // D
-    arrived(total(f_in), f_sem[1])
+    row_of = j * HH + c * part // D
+    f_mate = slots("r", 1)
+    f_own = f_in.at[j, pl.ds(0, nc - 1)]
+    arrived(f_own, f_sem[1])
+    remote(f_in.at[j], f_in.at[j], f_mate, mate)
+    arrived(f_in.at[1 - j], f_mate)
     arrived(total(l_in), l_sem[1])
 
     def scan(src, dst, reverse):
         def one(n, run):
             chip = nc - 1 - n if reverse else n
             dst[pl.ds(chip, 1)] = run.astype(BF16)[None]
-            fade = jnp.exp(f_in[pl.ds(chip, 1), pl.ds(head_of, 1), :][0])
+            fade = jnp.exp(
+                f_in[0, pl.ds(chip, 1), pl.ds(row_of, 1), :][0]
+                + f_in[1, pl.ds(chip, 1), pl.ds(row_of, 1), :][0]
+            )
             return fade * run + src[pl.ds(chip, 1)][0].astype(F32)
 
         lax.fori_loop(0, nc, one, jnp.zeros((part, D), F32), unroll=True)
@@ -413,6 +419,9 @@
         copy = pltpu.make_async_copy(outs.at[n, j], ref.at[:, mine], lsem.at[9 + n])
         copy.start()
         out_local.append(copy)
+        emit_far(n, ref)
+
+    def emit_far(n, ref):
         far = pltpu.make_async_remote_copy(
             src_ref=outs.at[n, 1 - j], dst_ref=ref.at[:, mine], send_sem=ssem.at[slots("s", 1)],
             recv_sem=rsem.at[out_r + n], device_id=mate, device_id_type=MESH,
@@ -498,20 +507,30 @@
     during("b")
 
     arrived(b_in.at[pl.ds(0, 512 - part)], b_sem[1])
-    for h in range(HH):
-        state = b_in[h * D : (h + 1) * D, :]
-        weight = cols[:, 8 + h : 9 + h]
-        put(2, h, dk[h] + weight * nt(head(vb, 2, h), state))
-    emit(2, ok_ref)
-    for h in range(HH):
-        state = b_in[h * D : (h + 1) * D, :]
-        weight = cols[:, 8 + h : 9 + h]
-        put(3, h, dv[h] + weight * nn(head(kb, 2, h), state))
-    emit(3, ov_ref)
+    def finish(block, store):
+        at = pl.ds(pl.multiple_of(block * D, D), D)
+        for h in range(HH):
+            cut = slice(h * D, (h + 1) * D)
+            state = b_in[cut, :]
+            weight = cols[at, 8 + h : 9 + h]
+            store(2, h, dk[h, at, :] + weight * nt(vb[2, block, :, cut], state))
+            store(3, h, dv[h, at, :] + weight * nn(kb[2, block, :, cut], state))
+
+    def for_mate(n, h, value):
+        outs[n, 1 - j, :, h * D : (h + 1) * D] = value.astype(BF16)
+
+    def for_here(n, h, value):
+        ref = (ok_ref, ov_ref)[n - 2]
+        ref[:, pl.ds(pl.multiple_of(j * HW + h * D, D), D)] = value.astype(BF16)
+
+    finish(1 - j, for_mate)
+    emit_far(2, ok_ref)
+    emit_far(3, ov_ref)
+    finish(j, for_here)
 
     for copy, _ in sends:
         copy.wait_send()
-    pltpu.make_async_copy(total(f_in), total(f_in), ssem.at[f_sem[0]]).wait()
+    pltpu.make_async_copy(f_own, f_own, ssem.at[f_sem[0]]).wait()
     for ref, sem in ((l_in, l_sem), (e_out, e_sem), (o_in, o_sem), (b_out, b_sem)):
         pltpu.make_async_copy(total(ref), total(ref), ssem.at[sem[0]]).wait()
     rest_x = xs.at[pl.ds(0, 2 * nx - 1)]
@@ -557,7 +576,7 @@
             scratch_shapes=[
                 band, band, band, band, pltpu.VMEM((D, HW), BF16), pltpu.VMEM((D, HW), BF16),
                 tile2, tile2, tile2, pltpu.VMEM((1, 5), jnp.int32),
-                pltpu.VMEM((HW, D), F32), pltpu.VMEM((2, HW, D), F32), pltpu.VMEM((nc, 8, D), F32),
+                pltpu.VMEM((HW, D), F32), pltpu.VMEM((2, HW, D), F32), pltpu.VMEM((2, nc, 8, D), F32),
                 whole, share, share, whole,
                 share, whole, share, whole,
                 pltpu.VMEM((2 * nx, 8, T2), F32), pltpu.VMEM((3, 24, T2), F32),

time: 58.8 us -> 57.9 us (0.985)
  Pallas kernels: 58 us -> 57.2 us
    pallas_call x1, Pallas kernels: 57 us -> 56.2 us  [body(): pl.pallas_call(functools.partial(kernel, nc, nx), name='mixer', out_shape...]
where the time goes in v4:
time: 57.9 us; the launch traced here: 57.8 us
  Pallas kernels  57.2 us (99%)
  between operations  0.64 us (1%)
    pallas_call x1, Pallas kernels, body(): pl.pallas_call(functools.partial(kernel, nc, nx), name='mixer', out_shape...  56.2 us

profile of v4, /device:TPU:1, one launch (start us, length us, event | category | flops | bytes accessed | tf_op | source)
XLA Modules:
  0.0 57.8 jit_solution(942585968915325573)
XLA Ops:
  0.6 56.2 %mixer.1 = (bf16[128,1024]{1,0:T(8,128)(2,1)S(1)}, bf16[128,1024]{1,0:T(8,128)(2,1)S(1)}, bf16[128,1024]{1,0:T(8,128)(2,1)S(1)}, bf16[128,1024]{1,0:T(8,128)(2,1)S(1)}) custom-call(bf16[128,1024]{1,0:T(8,128)(2,1)} %q_ref.1, bf16[128,1024]{1,0:T(8,128)(2,1)} %k_ref.1, bf16[128,1024]{1,0:T(8,128)(2,1)} %v_ref.1, bf16[128,1024]{1,0:T(8,128)(2,1)} %g_ref.1, ...), custom_call_target="tpu_custom_call" | custom-call | tf_op jit(solution)/shard_map/mixer/pallas_call | solution.py:570
  56.8 1.0 %store.1 = (bf16[128,1024]{1,0:T(8,128)(2,1)}, bf16[128,1024]{1,0:T(8,128)(2,1)}, bf16[128,1024]{1,0:T(8,128)(2,1)}, bf16[128,1024]{1,0:T(8,128)(2,1)}) custom-call(bf16[128,1024]{1,0:T(8,128)(2,1)S(1)} %get-tuple-element.8.a, bf16[128,1024]{1,0:T(8,128)(2,1)S(1)} %get-tuple-element.9.b, bf16[128,1024]{1,0:T(8,128)(2,1)S(1)} %get-tuple-element.10.c, ...), custom_call_target="tpu_custom_call" | custom-call | tf_op jit(solution)/shard_map/store/pallas_call | solution.py:604

commit v5 on v4

--- a/solution.py
+++ b/solution.py
@@ -22,9 +22,9 @@
 PLAN = {
     "p": ("k1a", "q1a"),
     "l": ("k1b", "q1b", "v1a", "g1a", "intra"),
-    "e": ("v1b", "g1b", "k2a", "q2a", "k2b", "q2b"),
-    "x": ("v2a", "g2a"),
-    "o": ("v2b", "g2b", "soft", "ssd"),
+    "e": ("v1b", "g1b", "k2a", "k2b", "q2a"),
+    "x": ("v2a", "q2b"),
+    "o": ("v2b", "g2a", "g2b", "soft", "ssd"),
     "b": ("query", "early", "late"),
 }
 
@@ -71,9 +71,8 @@
 
     lax.fori_loop(0, nc - 1, greet, 0)
     greeted = nc - 1
-    for other in (dev(c + 1, 1 - j, x), dev(c + nc - 1, 1 - j, x), dev(c, 1 - j, x)):
-        pl.semaphore_signal(barrier, 1, device_id=other, device_id_type=MESH)
-        greeted += 1
+    pl.semaphore_signal(barrier, 1, device_id=dev(c, 1 - j, x), device_id_type=MESH)
+    greeted += 1
     for step in range(1, nx):
         for core in range(2):
             pl.semaphore_signal(
@@ -189,41 +188,46 @@
     swap_send(2, q_ref.at[:, other_half], qb, 0)
     swap_send(3, g_ref.at[:, other_half], gb, 0)
 
-    first = slots("r", 16)
-    second = slots("r", 16)
+    first = slots("r", 8)
+    second = slots("r", 8)
     ways = {
-        "k": (0, k_ref, kb, 0, 1), "q": (1, q_ref, qb, 2, nc - 1),
-        "v": (2, v_ref, vb, 0, 1), "g": (3, g_ref, gb, 2, nc - 1),
+        "k": (0, k_ref, kb, 2, 0, 1), "v": (1, v_ref, vb, 2, 0, 1),
+        "q": (2, q_ref, qb, 0, 2, nc - 1), "g": (3, g_ref, gb, 0, 2, nc - 1),
     }
-
-    def half(name):
-        at = 4 * ways[name[0]][0] + 2 * (name[2] == "b")
-        return pl.ds(64 * (name[2] == "b"), 64), first + at, second + at
+    swapped = set()
+
+    def have(name):
+        n, _, buf, slot, _, _ = ways[name]
+        if name not in swapped:
+            swapped.add(name)
+            arrived(buf.at[slot, 1 - j], swap + n)
+
+    def place(name):
+        mates = name[2] == "b"
+        at = 2 * ways[name[0]][0] + mates
+        return (1 - j if mates else j), first + at, second + at
 
     def own_on(name):
-        _, src, dst, _, step = ways[name[0]]
-        lines, near, _ = half(name)
-        for core in range(2):
-            remote(
-                src.at[lines, pl.ds(core * HW, HW)], dst.at[1, j, lines], near + j,
-                dev(c + step, core, x),
-            )
+        _, src, buf, slot, _, step = ways[name[0]]
+        block, near, _ = place(name)
+        if name[2] == "b":
+            have(name[0])
+            src = buf.at[slot, block]
+        else:
+            src = src.at[:, mine]
+        remote(src, buf.at[1, block], near, dev(c + step, j, x))
 
     def hand_on(name):
-        _, _, buf, far, step = ways[name[0]]
-        lines, near, later = half(name)
-        for core in range(2):
-            arrived(buf.at[1, core, lines], near + core)
-            remote(
-                buf.at[1, core, lines], buf.at[far, core, lines], later + core, dev(c + step, j, x)
-            )
+        _, _, buf, _, far, step = ways[name[0]]
+        block, near, later = place(name)
+        arrived(buf.at[1, block], near)
+        remote(buf.at[1, block], buf.at[far, block], later, dev(c + step, j, x))
 
     def landed(name):
-        _, _, buf, far, _ = ways[name]
+        _, _, buf, _, far, _ = ways[name]
         for end in "ab":
-            lines, _, later = half(name + "2" + end)
-            for core in range(2):
-                arrived(buf.at[far, core, lines], later + core)
+            block, _, later = place(name + "2" + end)
+            arrived(buf.at[far, block], later)
 
     acts = {}
 
@@ -279,10 +283,8 @@
 
         for copy in local[7:9]:
             copy.wait()
-        arrived(kb.at[2, 1 - j], swap)
-        arrived(vb.at[2, 1 - j], swap + 1)
-        arrived(qb.at[0, 1 - j], swap + 2)
-        arrived(gb.at[0, 1 - j], swap + 3)
+        for name in ways:
+            have(name)
         for h in range(HH):
             q, k, v = head(qb, 0, h), head(kb, 2, h), head(vb, 2, h)
             p_row, p_col = rows[h : h + 1, :], cols[:, h : h + 1]

time: 57.9 us -> 59.1 us (1.021)
  the two profiles are of different devices: /device:TPU:1 before, /device:TPU:23 now
where the time goes in v5:
time: 59.1 us; the launch traced here: 59 us
  Pallas kernels  58.4 us (99%)
  between operations  0.64 us (1%)
    pallas_call x1, Pallas kernels, body(): pl.pallas_call(functools.partial(kernel, nc, nx), name='mixer', out_shape...  57.4 us

profile of v5, /device:TPU:23, one launch (start us, length us, event | category | flops | bytes accessed | tf_op | source)
XLA Modules:
  0.0 59.0 jit_solution(8591409506921673019)
XLA Ops:
  0.6 57.4 %mixer.1 = (bf16[128,1024]{1,0:T(8,128)(2,1)S(1)}, bf16[128,1024]{1,0:T(8,128)(2,1)S(1)}, bf16[128,1024]{1,0:T(8,128)(2,1)S(1)}, bf16[128,1024]{1,0:T(8,128)(2,1)S(1)}) custom-call(bf16[128,1024]{1,0:T(8,128)(2,1)} %q_ref.1, bf16[128,1024]{1,0:T(8,128)(2,1)} %k_ref.1, bf16[128,1024]{1,0:T(8,128)(2,1)} %v_ref.1, bf16[128,1024]{1,0:T(8,128)(2,1)} %g_ref.1, ...), custom_call_target="tpu_custom_call" | custom-call | tf_op jit(solution)/shard_map/mixer/pallas_call | solution.py:572
  58.0 1.0 %store.1 = (bf16[128,1024]{1,0:T(8,128)(2,1)}, bf16[128,1024]{1,0:T(8,128)(2,1)}, bf16[128,1024]{1,0:T(8,128)(2,1)}, bf16[128,1024]{1,0:T(8,128)(2,1)}) custom-call(bf16[128,1024]{1,0:T(8,128)(2,1)S(1)} %get-tuple-element.8.a, bf16[128,1024]{1,0:T(8,128)(2,1)S(1)} %get-tuple-element.9.b, bf16[128,1024]{1,0:T(8,128)(2,1)S(1)} %get-tuple-element.10.c, ...), custom_call_target="tpu_custom_call" | custom-call | tf_op jit(solution)/shard_map/store/pallas_call | solution.py:606

commit v6 on v5

--- a/solution.py
+++ b/solution.py
@@ -22,9 +22,9 @@
 PLAN = {
     "p": ("k1a", "q1a"),
     "l": ("k1b", "q1b", "v1a", "g1a", "intra"),
-    "e": ("v1b", "g1b", "k2a", "k2b", "q2a"),
-    "x": ("v2a", "q2b"),
-    "o": ("v2b", "g2a", "g2b", "soft", "ssd"),
+    "e": ("v1b", "g1b", "k2a", "q2a", "k2b", "q2b"),
+    "x": ("v2a", "g2a"),
+    "o": ("v2b", "g2b", "soft", "ssd"),
     "b": ("query", "early", "late"),
 }
 

time: 59.1 us -> 57.8 us (0.978)
  the two profiles are of different devices: /device:TPU:23 before, /device:TPU:1 now
where the time goes in v6:
time: 57.8 us; the launch traced here: 57.7 us
  Pallas kernels  57.1 us (99%)
  between operations  0.64 us (1%)
    pallas_call x1, Pallas kernels, body(): pl.pallas_call(functools.partial(kernel, nc, nx), name='mixer', out_shape...  56.1 us

profile of v6, /device:TPU:1, one launch (start us, length us, event | category | flops | bytes accessed | tf_op | source)
XLA Modules:
  0.0 57.7 jit_solution(5407210244048920757)
XLA Ops:
  0.6 56.1 %mixer.1 = (bf16[128,1024]{1,0:T(8,128)(2,1)S(1)}, bf16[128,1024]{1,0:T(8,128)(2,1)S(1)}, bf16[128,1024]{1,0:T(8,128)(2,1)S(1)}, bf16[128,1024]{1,0:T(8,128)(2,1)S(1)}) custom-call(bf16[128,1024]{1,0:T(8,128)(2,1)} %q_ref.1, bf16[128,1024]{1,0:T(8,128)(2,1)} %k_ref.1, bf16[128,1024]{1,0:T(8,128)(2,1)} %v_ref.1, bf16[128,1024]{1,0:T(8,128)(2,1)} %g_ref.1, ...), custom_call_target="tpu_custom_call" | custom-call | tf_op jit(solution)/shard_map/mixer/pallas_call | solution.py:572
  56.7 1.0 %store.1 = (bf16[128,1024]{1,0:T(8,128)(2,1)}, bf16[128,1024]{1,0:T(8,128)(2,1)}, bf16[128,1024]{1,0:T(8,128)(2,1)}, bf16[128,1024]{1,0:T(8,128)(2,1)}) custom-call(bf16[128,1024]{1,0:T(8,128)(2,1)S(1)} %get-tuple-element.8.a, bf16[128,1024]{1,0:T(8,128)(2,1)S(1)} %get-tuple-element.9.b, bf16[128,1024]{1,0:T(8,128)(2,1)S(1)} %get-tuple-element.10.c, ...), custom_call_target="tpu_custom_call" | custom-call | tf_op jit(solution)/shard_map/store/pallas_call | solution.py:606

commit v7 on v6

--- a/solution.py
+++ b/solution.py
@@ -45,7 +45,7 @@
     nc, nx,
     q_ref, k_ref, v_ref, g_ref, ld_ref, st_ref, bm_ref,
     om_ref, oq_ref, ok_ref, ov_ref,
-    kb, vb, qb, gb, kx, vx, ldb, stb, mk, bmv, part_out, part_in, f_in, l_out, l_in, e_out, e_in,
+    kb, vb, qb, gb, kx, vx, ldb, stb, mk, bmv, part_out, part_in, part_own, f_in, l_out, l_in, e_out, e_in,
     o_in, o_out, b_out, b_in, xs, stat, rows, cols, bias, big,
     mix, mixt, pairt, qt, ssd, dss, wq, wk, dq, dk, dv, outs,
     ssem, rsem, lsem,
@@ -163,8 +163,8 @@
         cut = slice(h * D, (h + 1) * D)
         part_out[cut, :] = tn(
             (carry_mate[:, h : h + 1] * kx[:, cut].astype(F32)).astype(BF16), vx[:, cut]
-        )
-        part_in[j, cut, :] = tn(
+        ).astype(BF16)
+        part_own[cut, :] = tn(
             (carry_mine[:, h : h + 1] * kb[2, j, :, cut].astype(F32)).astype(BF16),
             vb[2, j, :, cut],
         )
@@ -175,7 +175,7 @@
     small = slots("r", 4)
     remote(ldb.at[j], ldb.at[j], small, mate)
     remote(stb.at[j], stb.at[j], small + 1, mate)
-    remote(part_out, part_in.at[j], small + 2, mate)
+    remote(part_out, part_in, small + 2, mate)
     remote(mk.at[j], mk.at[j], small + 3, mate)
     f_sem = exchange(lambda chip: f_in.at[j, c], lambda sender: f_in.at[j, sender])
     swap = slots("r", 4)
@@ -251,10 +251,14 @@
     decay, step_row = pair
 
     fade_late = jnp.exp(jnp.sum(decay[:, D : 2 * D], axis=1, keepdims=True))
-    arrived(part_in.at[1 - j], small + 2)
+    arrived(part_in, small + 2)
+    of_own, of_mate = jnp.where(low, fade_late, 1.0), jnp.where(low, 1.0, fade_late)
     for h in range(HH):
         cut = slice(h * D, (h + 1) * D)
-        l_out[cut, :] = (fade_late[h : h + 1, :] * part_in[0, cut, :] + part_in[1, cut, :]).astype(BF16)
+        l_out[cut, :] = (
+            of_own[h : h + 1, :] * part_own[cut, :]
+            + of_mate[h : h + 1, :] * part_in[cut, :].astype(F32)
+        ).astype(BF16)
     l_sem = exchange(lambda chip: l_out.at[own(chip)], lambda sender: l_in.at[sender])
     l_in[pl.ds(c, 1)] = l_out[own(c), :][None]
 
@@ -578,7 +582,7 @@
             scratch_shapes=[
                 band, band, band, band, pltpu.VMEM((D, HW), BF16), pltpu.VMEM((D, HW), BF16),
                 tile2, tile2, tile2, pltpu.VMEM((1, 5), jnp.int32),
-                pltpu.VMEM((HW, D), F32), pltpu.VMEM((2, HW, D), F32), pltpu.VMEM((2, nc, 8, D), F32),
+                whole, whole, pltpu.VMEM((HW, D), F32), pltpu.VMEM((2, nc, 8, D), F32),
                 whole, share, share, whole,
                 share, whole, share, whole,
                 pltpu.VMEM((2 * nx, 8, T2), F32), pltpu.VMEM((3, 24, T2), F32),

time: 57.8 us -> 57.7 us (level)
  no operation moved by 1% of the time
where the time goes in v7:
time: 57.7 us; the launch traced here: 57.6 us
  Pallas kernels  57 us (99%)
  between operations  0.64 us (1%)
    pallas_call x1, Pallas kernels, body(): pl.pallas_call(functools.partial(kernel, nc, nx), name='mixer', out_shape...  56 us

profile of v7, /device:TPU:1, one launch (start us, length us, event | category | flops | bytes accessed | tf_op | source)
XLA Modules:
  0.0 57.6 jit_solution(9703151246967099505)
XLA Ops:
  0.6 56.0 %mixer.1 = (bf16[128,1024]{1,0:T(8,128)(2,1)S(1)}, bf16[128,1024]{1,0:T(8,128)(2,1)S(1)}, bf16[128,1024]{1,0:T(8,128)(2,1)S(1)}, bf16[128,1024]{1,0:T(8,128)(2,1)S(1)}) custom-call(bf16[128,1024]{1,0:T(8,128)(2,1)} %q_ref.1, bf16[128,1024]{1,0:T(8,128)(2,1)} %k_ref.1, bf16[128,1024]{1,0:T(8,128)(2,1)} %v_ref.1, bf16[128,1024]{1,0:T(8,128)(2,1)} %g_ref.1, ...), custom_call_target="tpu_custom_call" | custom-call | tf_op jit(solution)/shard_map/mixer/pallas_call | solution.py:576
  56.6 1.0 %store.1 = (bf16[128,1024]{1,0:T(8,128)(2,1)}, bf16[128,1024]{1,0:T(8,128)(2,1)}, bf16[128,1024]{1,0:T(8,128)(2,1)}, bf16[128,1024]{1,0:T(8,128)(2,1)}) custom-call(bf16[128,1024]{1,0:T(8,128)(2,1)S(1)} %get-tuple-element.8.a, bf16[128,1024]{1,0:T(8,128)(2,1)S(1)} %get-tuple-element.9.b, bf16[128,1024]{1,0:T(8,128)(2,1)S(1)} %get-tuple-element.10.c, ...), custom_call_target="tpu_custom_call" | custom-call | tf_op jit(solution)/shard_map/store/pallas_call | solution.py:610
